TPU v7x, 32 devices: a whole 2x2x4 slice. The times are simulated.
32 devices in a mesh: crops: 2 (over y), row: 4 (over z), sub: 2 (over x), pair: 2 (over core).
Axes of the slice: x: 2, y: 2, z: 4, core: 2. Of those that a mesh axis runs over, the one named last changes fastest.
Arguments:
- pair_act: bfloat16 [64, 32, 128], P(('crops', 'row'), ('sub', 'pair')), parts along dimension 0, may hold values from -6 to 6
- residue_mask: int32 [64], P('crops'), parts along dimension 0, may hold values 0 or 1
- w_proj: bfloat16 [128, 512], replicated, may hold values from -0.5 to 0.5
- w_gate: bfloat16 [128, 128], replicated, may hold values from -0.5 to 0.5
- w_out: bfloat16 [128, 128], replicated, may hold values from -0.5 to 0.5
- d_transposed: bfloat16 [64, 32, 128], P(('crops', 'row', 'sub', 'pair')), parts along dimension 0, may hold values from -6 to 6
Outputs:
- transposed: bfloat16 [64, 32, 128], P(('crops', 'row', 'sub', 'pair')), parts along dimension 0
- d_pair: bfloat16 [64, 32, 128], P(('crops', 'row'), ('sub', 'pair')), parts along dimension 0
- g_proj: float32 [256, 512], P('crops'), parts along dimension 0
- g_gate: float32 [256, 128], P('crops'), parts along dimension 0
- g_out: float32 [256, 128], P('crops'), parts along dimension 0
There are 2 independent parts, one for each index of `crops`. A program takes and returns all parts, laid end to end along the dimension named above; an argument that names none is the same for every part. Nothing has to cross between parts.
All inputs are finite; a program needn't handle non-finite values.
Results may differ from a plain program's by a relative error of at most 0.0088.
Values may be sent and summed in bfloat16 or wider, within the bound.
A program may use at most 64 MiB of HBM per device.

v0:
```python
import jax
import jax.numpy as jnp
from jax import lax
from jax.sharding import PartitionSpec as P

epsilon = 1e-05


def layer_norm(values):
    row_mean = jnp.mean(values, axis=-1, keepdims=True)
    centred = values - row_mean
    row_var = jnp.mean(centred * centred, axis=-1, keepdims=True)
    return centred * lax.rsqrt(row_var + epsilon)


def norm_back(values, cotangent):
    return jax.vjp(layer_norm, values)[1](cotangent)[0]


def front_forward(pair_rows, w_proj, w_gate, pair_mask):
    hidden_width = w_proj.shape[1] // 4
    normed = layer_norm(pair_rows).astype(jnp.bfloat16)
    projected = jnp.dot(normed, w_proj, preferred_element_type=jnp.float32)
    gate_pre = jnp.dot(normed, w_gate, preferred_element_type=jnp.float32)
    left_b = (
        jax.nn.sigmoid(projected[:, :hidden_width])
        * projected[:, hidden_width : 2 * hidden_width]
        * pair_mask
    )
    right_b = (
        jax.nn.sigmoid(projected[:, 2 * hidden_width : 3 * hidden_width])
        * projected[:, 3 * hidden_width :]
        * pair_mask
    )
    return (
        normed,
        projected,
        left_b.astype(jnp.bfloat16),
        right_b.astype(jnp.bfloat16),
        jax.nn.sigmoid(gate_pre),
    )


def back_forward(crossed_rows, gate_act, pair_rows, w_out):
    normed_x = layer_norm(crossed_rows.astype(jnp.float32)).astype(jnp.bfloat16)
    out_proj = jnp.dot(normed_x, w_out, preferred_element_type=jnp.float32)
    return (normed_x, out_proj, pair_rows + gate_act * out_proj)


def back_backward(crossed_rows, out_proj, gate_act, w_out, d_up):
    d_out_b = (gate_act * d_up).astype(jnp.bfloat16)
    d_gate_b = (out_proj * d_up * gate_act * (1.0 - gate_act)).astype(jnp.bfloat16)
    d_normed_x = jnp.dot(d_out_b, w_out.T, preferred_element_type=jnp.float32)
    d_cross_b = norm_back(crossed_rows.astype(jnp.float32), d_normed_x).astype(jnp.bfloat16)
    return (d_out_b, d_gate_b, d_cross_b)


def front_backward(
    pair_rows, projected, pair_mask, d_left, d_right, d_gate_b, w_proj, w_gate, d_up
):
    hidden_width = w_proj.shape[1] // 4
    left_gate = jax.nn.sigmoid(projected[:, :hidden_width])
    left_value = projected[:, hidden_width : 2 * hidden_width]
    right_gate = jax.nn.sigmoid(projected[:, 2 * hidden_width : 3 * hidden_width])
    right_value = projected[:, 3 * hidden_width :]
    d_proj = jnp.concatenate(
        [
            d_left * left_value * pair_mask * left_gate * (1.0 - left_gate),
            d_left * left_gate * pair_mask,
            d_right * right_value * pair_mask * right_gate * (1.0 - right_gate),
            d_right * right_gate * pair_mask,
        ],
        axis=1,
    ).astype(jnp.bfloat16)
    d_normed = jnp.dot(d_proj, w_proj.T, preferred_element_type=jnp.float32) + jnp.dot(
        d_gate_b, w_gate.T, preferred_element_type=jnp.float32
    )
    d_pair = (d_up + norm_back(pair_rows, d_normed)).astype(jnp.bfloat16)
    return (d_proj, d_pair)


def to_channels(stacked, row_block, col_block):
    groups = stacked.shape[0]
    col_groups = lax.axis_size(("sub", "pair"))
    sectioning = stacked[None]
    arrived = lax.all_to_all(sectioning, ("sub", "pair"), split_axis=2, concat_axis=0, tiled=True)
    channel_share = arrived.shape[2]
    arrived = arrived.reshape(col_groups, groups, channel_share, row_block, col_block)
    return arrived.transpose(1, 2, 3, 0, 4).reshape(
        groups, channel_share, row_block, col_groups * col_block
    )


def from_channels(stacked, row_block, col_block):
    groups = stacked.shape[0]
    arrived = lax.all_to_all(stacked, ("sub", "pair"), split_axis=3, concat_axis=1, tiled=True)
    return arrived.transpose(0, 2, 3, 1).reshape(groups, row_block * col_block, arrived.shape[1])


def on_device(pair_act, residue_mask, w_proj, w_gate, w_out, d_transposed):
    row_block, col_block, channels = pair_act.shape
    row_count = lax.axis_size("row")
    col_groups = lax.axis_size(("sub", "pair"))
    crop_length = row_block * row_count
    block_width = col_block // row_count
    group_width = row_count // col_groups
    local_rows = row_block * col_block
    row_start = lax.axis_index("row") * row_block
    col_start = lax.axis_index(("sub", "pair")) * col_block
    row_valid = lax.dynamic_slice_in_dim(residue_mask, row_start, row_block, 0).astype(jnp.float32)
    col_valid = lax.dynamic_slice_in_dim(residue_mask, col_start, col_block, 0).astype(jnp.float32)
    pair_mask = (row_valid[:, None] * col_valid[None, :]).reshape(local_rows, 1)
    pair_rows = pair_act.reshape(local_rows, channels).astype(jnp.float32)
    normed, projected, left_b, right_b, gate_act = front_forward(
        pair_rows, w_proj, w_gate, pair_mask
    )
    paired = to_channels(jnp.stack([left_b.T, right_b.T]), row_block, col_block)
    left_t = paired[0]
    right_t = paired[1]
    crossed = jnp.einsum(
        "cik,cjk->cij",
        left_t,
        lax.all_gather(right_t, "row", axis=1, tiled=True),
        preferred_element_type=jnp.float32,
    )
    crossed_rows = from_channels(crossed.astype(jnp.bfloat16)[None], row_block, col_block)[0]
    normed_x, out_proj, updated = back_forward(crossed_rows, gate_act, pair_rows, w_out)
    updated_b = updated.astype(jnp.bfloat16).reshape(
        row_block, group_width, col_groups, block_width, channels
    )
    spread_cols = lax.all_to_all(
        updated_b, ("sub", "pair"), split_axis=2, concat_axis=2, tiled=True
    )
    regrouped = spread_cols.transpose(2, 1, 0, 3, 4).reshape(
        row_count, row_block, block_width, channels
    )
    turned = lax.all_to_all(regrouped, "row", split_axis=0, concat_axis=1, tiled=True)
    transposed = turned.reshape(crop_length, block_width, channels).transpose(1, 0, 2)
    back_in = d_transposed.transpose(1, 0, 2).reshape(row_count, row_block, block_width, channels)
    returned = lax.all_to_all(back_in, "row", split_axis=0, concat_axis=0, tiled=True)
    regrouped_back = returned.reshape(
        col_groups, group_width, row_block, block_width, channels
    ).transpose(2, 1, 0, 3, 4)
    restored = lax.all_to_all(
        regrouped_back, ("sub", "pair"), split_axis=2, concat_axis=2, tiled=True
    )
    d_up = restored.reshape(local_rows, channels).astype(jnp.float32)
    d_out_b, d_gate_b, d_cross_b = back_backward(crossed_rows, out_proj, gate_act, w_out, d_up)
    d_cross_t = to_channels(d_cross_b.T[None], row_block, col_block)[0]
    d_cross_cols = lax.all_to_all(d_cross_t, "row", split_axis=2, concat_axis=1, tiled=True)
    left_part = jnp.einsum(
        "cij,cjk->cik",
        d_cross_t,
        lax.all_gather(right_t, "row", axis=1, tiled=True),
        preferred_element_type=jnp.float32,
    )
    right_part = jnp.einsum(
        "cij,cik->cjk",
        d_cross_cols,
        lax.all_gather(left_t, "row", axis=1, tiled=True),
        preferred_element_type=jnp.float32,
    )
    d_rows_back = from_channels(
        jnp.stack([left_part, right_part]).astype(jnp.bfloat16), row_block, col_block
    )
    d_proj, d_pair = front_backward(
        pair_rows,
        projected,
        pair_mask,
        d_rows_back[0].astype(jnp.float32),
        d_rows_back[1].astype(jnp.float32),
        d_gate_b,
        w_proj,
        w_gate,
        d_up,
    )
    weight_terms = (
        jnp.einsum("rc,rd->cd", normed, d_proj, preferred_element_type=jnp.float32),
        jnp.einsum("rc,rd->cd", normed, d_gate_b, preferred_element_type=jnp.float32),
        jnp.einsum("rc,rd->cd", normed_x, d_out_b, preferred_element_type=jnp.float32),
    )
    g_proj, g_gate, g_out = lax.psum(
        (weight_terms[0], weight_terms[1], weight_terms[2]), ("row", "sub", "pair")
    )
    return (
        transposed,
        d_pair.reshape(row_block, col_block, channels),
        g_proj / crop_length,
        g_gate / crop_length,
        g_out / crop_length,
    )


def solution(mesh):
    in_specs = (
        P(("crops", "row"), ("sub", "pair"), None),
        P("crops"),
        P(),
        P(),
        P(),
        P(("crops", "row", "sub", "pair"), None, None),
    )
    out_specs = (
        P(("crops", "row", "sub", "pair"), None, None),
        P(("crops", "row"), ("sub", "pair"), None),
        P("crops", None),
        P("crops", None),
        P("crops", None),
    )
    return jax.shard_map(
        on_device, mesh=mesh, in_specs=in_specs, out_specs=out_specs, check_vma=False
    )
```

profile of v0, /device:TPU:0, one launch (start us, length us, event | category | flops | bytes accessed | tf_op | source)
XLA Modules:
  0.0 206.1 jit_solution(11747126363141678092)
XLA Ops:
  10.4 4.3 %all-to-all-start = ((bf16[4,2,2048]{2,1,0:T(2,128)(2,1)}), bf16[4,2,2048]{2,1,0:T(2,128)(2,1)S(1)}, u32[]{:S(2)}, u32[]{:S(2)}) async-start(bf16[4,2,2048]{2,1,0:T(2,128)(2,1)} %reshape.191), calls=%async_computation | async-start | bytes 65536 | tf_op jit(solution)/shard_map/all_to_all | solution.py:86
  15.4 3.3 %all-to-all-done = bf16[4,2,2048]{2,1,0:T(2,128)(2,1)S(1)} async-done(((bf16[4,2,2048]{2,1,0:T(2,128)(2,1)}), bf16[4,2,2048]{2,1,0:T(2,128)(2,1)S(1)}, u32[]{:S(2)}, u32[]{:S(2)}) %all-to-all-start) | async-done | bytes 32800 | tf_op jit(solution)/shard_map/all_to_all | solution.py:86
  18.7 5.3 %all-to-all-start.4 = ((bf16[4,8,2,128]{3,2,1,0:T(2,128)(2,1)}), bf16[4,8,2,128]{3,2,1,0:T(2,128)(2,1)}, u32[]{:S(2)}, u32[]{:S(2)}) async-start(bf16[4,8,2,128]{3,2,1,0:T(2,128)(2,1)} %bitcast.24), calls=%async_computation.4 | async-start | bytes 32768 | tf_op jit(solution)/shard_map/all_to_all | solution.py:140
  24.6 13.5 %all_gather.7 = bf16[32,32,32]{2,1,0:T(8,128)(2,1)S(1)} all-gather(bf16[32,8,32]{2,1,0:T(8,128)(2,1)S(1)} %copy.159), channel_id=1, replica_groups=mesh['crops'=2,'row'=4,'sub'=2,'pair'=2] {'row'}, dimensions={1}, use_global_device_ids=true | all-gather | bytes 81920 | tf_op jit(solution)/shard_map/all_gather | solution.py:123
  38.7 6.2 %all_to_all.96 = bf16[4,2,1024]{2,1,0:T(2,128)(2,1)S(1)} all-to-all(bf16[4,2,1024]{2,1,0:T(2,128)(2,1)S(1)} %reshape.193), channel_id=1, replica_groups=mesh['crops'=2,'row'=4,'sub'=2,'pair'=2] {'sub','pair'}, dimensions={0} | all-to-all | bytes 32768 | tf_op jit(solution)/shard_map/all_to_all | solution.py:96
  44.9 3.3 %all-to-all-start.5 = ((bf16[8,1,4,2,128]{4,3,0,1,2:T(2,128)(2,1)}), bf16[8,1,4,2,128]{4,3,0,1,2:T(2,128)(2,1)S(1)}, u32[]{:S(2)}, u32[]{:S(2)}) async-start(bf16[8,1,4,2,128]{4,3,0,1,2:T(2,128)(2,1)} %bitcast.27), calls=%async_computation.5 | async-start | bytes 32768 | tf_op jit(solution)/shard_map/all_to_all | solution.py:144
  48.7 3.2 %all-to-all-done.5 = bf16[8,1,4,2,128]{4,3,0,1,2:T(2,128)(2,1)S(1)} async-done(((bf16[8,1,4,2,128]{4,3,0,1,2:T(2,128)(2,1)}), bf16[8,1,4,2,128]{4,3,0,1,2:T(2,128)(2,1)S(1)}, u32[]{:S(2)}, u32[]{:S(2)}) %all-to-all-start.5) | async-done | bytes 16416 | tf_op jit(solution)/shard_map/all_to_all | solution.py:144
  54.9 0.8 reduce.4
  56.4 3.3 %all-to-all-start.6 = ((bf16[4,2,1024]{2,1,0:T(2,128)(2,1)}), bf16[4,2,1024]{2,1,0:T(2,128)(2,1)S(1)}, u32[]{:S(2)}, u32[]{:S(2)}) async-start(bf16[4,2,1024]{2,1,0:T(2,128)(2,1)} %reshape.195), calls=%async_computation.6 | async-start | bytes 32768 | tf_op jit(solution)/shard_map/all_to_all | solution.py:86
  59.7 13.0 %all_gather.8 = bf16[32,32,32]{2,1,0:T(8,128)(2,1)S(1)} all-gather(bf16[32,8,32]{2,1,0:T(8,128)(2,1)S(1)} %copy.160), channel_id=1, replica_groups=mesh['crops'=2,'row'=4,'sub'=2,'pair'=2] {'row'}, dimensions={1}, use_global_device_ids=true | all-gather | bytes 81920 | tf_op jit(solution)/shard_map/all_gather | solution.py:160
  73.3 3.9 %all-to-all-start.2 = ((bf16[8,1,4,2,128]{4,3,0,1,2:T(2,128)(2,1)}), bf16[8,1,4,2,128]{4,3,0,1,2:T(2,128)(2,1)}, u32[]{:S(2)}, u32[]{:S(2)}) async-start(bf16[8,1,4,2,128]{4,3,0,1,2:T(2,128)(2,1)} %copy.164), calls=%async_computation.2 | async-start | bytes 32768 | tf_op jit(solution)/shard_map/all_to_all | solution.py:131
  77.2 0.9 fusion.45
  79.3 1.8 all-to-all-done.2
  81.1 3.3 %all-to-all-start.7 = ((bf16[4,2,1024]{2,1,0:T(2,128)(2,1)}), bf16[4,2,1024]{2,1,0:T(2,128)(2,1)S(1)}, u32[]{:S(2)}, u32[]{:S(2)}) async-start(bf16[4,2,1024]{2,1,0:T(2,128)(2,1)} %reshape.197), calls=%async_computation.7 | async-start | bytes 32768 | tf_op jit(solution)/shard_map/all_to_all | solution.py:150
  84.5 5.4 %all-to-all-done.7 = bf16[4,2,1024]{2,1,0:T(2,128)(2,1)S(1)} async-done(((bf16[4,2,1024]{2,1,0:T(2,128)(2,1)}), bf16[4,2,1024]{2,1,0:T(2,128)(2,1)S(1)}, u32[]{:S(2)}, u32[]{:S(2)}) %all-to-all-start.7) | async-done | bytes 16416 | tf_op jit(solution)/shard_map/all_to_all | solution.py:150
  89.9 3.3 %all-to-all-start.3 = ((bf16[4,8,2,128]{3,2,1,0:T(2,128)(2,1)}), bf16[4,8,2,128]{3,2,1,0:T(2,128)(2,1)S(1)}, u32[]{:S(2)}, u32[]{:S(2)}) async-start(bf16[4,8,2,128]{3,2,1,0:T(2,128)(2,1)} %bitcast.20), calls=%async_computation.3 | async-start | bytes 32768 | tf_op jit(solution)/shard_map/all_to_all | solution.py:137
  93.9 0.8 reshape.199
  94.6 4.1 %all-to-all-done.3 = bf16[4,8,2,128]{3,2,1,0:T(2,128)(2,1)S(1)} async-done(((bf16[4,8,2,128]{3,2,1,0:T(2,128)(2,1)}), bf16[4,8,2,128]{3,2,1,0:T(2,128)(2,1)S(1)}, u32[]{:S(2)}, u32[]{:S(2)}) %all-to-all-start.3) | async-done | bytes 16416 | tf_op jit(solution)/shard_map/all_to_all | solution.py:137
  98.8 3.3 %all-to-all-start.8 = ((bf16[4,2,2048]{2,1,0:T(2,128)(2,1)}), bf16[4,2,2048]{2,1,0:T(2,128)(2,1)S(1)}, u32[]{:S(2)}, u32[]{:S(2)}) async-start(bf16[4,2,2048]{2,1,0:T(2,128)(2,1)} %reshape.199), calls=%async_computation.8 | async-start | bytes 65536 | tf_op jit(solution)/shard_map/all_to_all | solution.py:96
  102.1 0.9 fusion.47
  103.6 2.4 %all-to-all-done.8 = bf16[4,2,2048]{2,1,0:T(2,128)(2,1)S(1)} async-done(((bf16[4,2,2048]{2,1,0:T(2,128)(2,1)}), bf16[4,2,2048]{2,1,0:T(2,128)(2,1)S(1)}, u32[]{:S(2)}, u32[]{:S(2)}) %all-to-all-start.8) | async-done | bytes 32800 | tf_op jit(solution)/shard_map/all_to_all | solution.py:96
  106.6 1.0 fusion.40
  108.8 88.0 %all-reduce.3.cloned.1.call-done = (f32[128,512]{1,0:T(8,128)}, f32[128,128]{1,0:T(8,128)}, f32[128,128]{1,0:T(8,128)}) async-done(((f32[128,512]{1,0:T(8,128)}, f32[128,128]{1,0:T(8,128)}, f32[128,128]{1,0:T(8,128)}), (f32[128,512]{1,0:T(8,128)}, f32[128,128]{1,0:T(8,128)}, f32[128,128]{1,0:T(8,128)})) %all-reduce.3.cloned.1.call-update) | async-done | bytes 393232 | tf_op jit(solution)/shard_map/psum | solution.py:182
  196.8 1.7 broadcast_multiply_fusion
  (97 shorter events, 14.8 us)
Async XLA Ops:
  7.2 2.1 %copy-start = (bf16[128,512]{1,0:T(8,128)(2,1)S(1)}, bf16[128,512]{1,0:T(8,128)(2,1)}, u32[]{:S(2)}) copy-start(bf16[128,512]{1,0:T(8,128)(2,1)} %param.8) | copy-start | bytes 393220
  7.2 0.8 copy-start.1
  8.3 0.7 copy-start.7
  10.4 4.3 %copy-start.6 = (bf16[2,32,128]{2,1,0:T(8,128)(2,1)S(1)}, bf16[2,32,128]{2,1,0:T(8,128)(2,1)}, u32[]{:S(2)}) copy-start(bf16[2,32,128]{2,1,0:T(8,128)(2,1)} %param.11) | copy-start | bytes 49156
  10.4 8.3 %all-to-all-start = ((bf16[4,2,2048]{2,1,0:T(2,128)(2,1)}), bf16[4,2,2048]{2,1,0:T(2,128)(2,1)S(1)}, u32[]{:S(2)}, u32[]{:S(2)}) async-start(bf16[4,2,2048]{2,1,0:T(2,128)(2,1)} %reshape.191), calls=%async_computation | async-start | bytes 65536 | tf_op jit(solution)/shard_map/all_to_all | solution.py:86
  18.7 19.9 %all-to-all-start.4 = ((bf16[4,8,2,128]{3,2,1,0:T(2,128)(2,1)}), bf16[4,8,2,128]{3,2,1,0:T(2,128)(2,1)}, u32[]{:S(2)}, u32[]{:S(2)}) async-start(bf16[4,8,2,128]{3,2,1,0:T(2,128)(2,1)} %bitcast.24), calls=%async_computation.4 | async-start | bytes 32768 | tf_op jit(solution)/shard_map/all_to_all | solution.py:140
  44.9 7.1 %all-to-all-start.5 = ((bf16[8,1,4,2,128]{4,3,0,1,2:T(2,128)(2,1)}), bf16[8,1,4,2,128]{4,3,0,1,2:T(2,128)(2,1)S(1)}, u32[]{:S(2)}, u32[]{:S(2)}) async-start(bf16[8,1,4,2,128]{4,3,0,1,2:T(2,128)(2,1)} %bitcast.27), calls=%async_computation.5 | async-start | bytes 32768 | tf_op jit(solution)/shard_map/all_to_all | solution.py:144
  51.9 0.8 copy-start.4
  52.7 0.8 copy-start.5
  56.4 16.9 %all-to-all-start.6 = ((bf16[4,2,1024]{2,1,0:T(2,128)(2,1)}), bf16[4,2,1024]{2,1,0:T(2,128)(2,1)S(1)}, u32[]{:S(2)}, u32[]{:S(2)}) async-start(bf16[4,2,1024]{2,1,0:T(2,128)(2,1)} %reshape.195), calls=%async_computation.6 | async-start | bytes 32768 | tf_op jit(solution)/shard_map/all_to_all | solution.py:86
  73.3 7.8 %all-to-all-start.2 = ((bf16[8,1,4,2,128]{4,3,0,1,2:T(2,128)(2,1)}), bf16[8,1,4,2,128]{4,3,0,1,2:T(2,128)(2,1)}, u32[]{:S(2)}, u32[]{:S(2)}) async-start(bf16[8,1,4,2,128]{4,3,0,1,2:T(2,128)(2,1)} %copy.164), calls=%async_computation.2 | async-start | bytes 32768 | tf_op jit(solution)/shard_map/all_to_all | solution.py:131
  81.1 8.8 %all-to-all-start.7 = ((bf16[4,2,1024]{2,1,0:T(2,128)(2,1)}), bf16[4,2,1024]{2,1,0:T(2,128)(2,1)S(1)}, u32[]{:S(2)}, u32[]{:S(2)}) async-start(bf16[4,2,1024]{2,1,0:T(2,128)(2,1)} %reshape.197), calls=%async_computation.7 | async-start | bytes 32768 | tf_op jit(solution)/shard_map/all_to_all | solution.py:150
  89.9 8.8 %all-to-all-start.3 = ((bf16[4,8,2,128]{3,2,1,0:T(2,128)(2,1)}), bf16[4,8,2,128]{3,2,1,0:T(2,128)(2,1)S(1)}, u32[]{:S(2)}, u32[]{:S(2)}) async-start(bf16[4,8,2,128]{3,2,1,0:T(2,128)(2,1)} %bitcast.20), calls=%async_computation.3 | async-start | bytes 32768 | tf_op jit(solution)/shard_map/all_to_all | solution.py:137
  98.8 7.2 %all-to-all-start.8 = ((bf16[4,2,2048]{2,1,0:T(2,128)(2,1)}), bf16[4,2,2048]{2,1,0:T(2,128)(2,1)S(1)}, u32[]{:S(2)}, u32[]{:S(2)}) async-start(bf16[4,2,2048]{2,1,0:T(2,128)(2,1)} %reshape.199), calls=%async_computation.8 | async-start | bytes 65536 | tf_op jit(solution)/shard_map/all_to_all | solution.py:96
  102.0 94.8 %all-reduce.3.cloned.1.call-start = ((), (), s32[]{:S(2)}) async-start(), calls=%async_computation.9 | async-start | bytes 786432 | tf_op jit(solution)/shard_map/psum | solution.py:182
  196.8 1.7 copy-start.2
  196.8 1.7 copy-start.3
Sparse Core Ops, SparseCore 0:
  108.2 88.5 all-reduce.2
where the time goes:
time: 207 us; the launch traced here: 206 us
  waiting for transfers between devices  108 us (52%)
  blocking collectives  32.7 us (16%)
  starting transfers between devices  29.9 us (14%)
  between operations  14.4 us (7%)
  local copies, waits for them, and re-layouts  10.9 us (5%)
  other arithmetic  5.28 us (3%)
  matrix products  4.67 us (2%)
    psum x1, waiting for transfers between devices, on_device(): lax.psum((weight_terms[0], weight_terms[1], weight_terms[2]), ('row', 'su...  88 us
    all_gather x1, blocking collectives, on_device(): lax.all_gather(right_t, 'row', axis=1, tiled=True)  13.5 us
    all_gather x1, blocking collectives, on_device(): lax.all_gather(left_t, 'row', axis=1, tiled=True)  13 us
    all_to_all x2, starting transfers between devices, to_channels(): lax.all_to_all(sectioning, ('sub', 'pair'), split_axis=2, concat_axis=0,...  7.59 us
    unnamed x27, local copies, waits for them, and re-layouts  6.74 us
    all_to_all x1, blocking collectives, from_channels(): lax.all_to_all(stacked, ('sub', 'pair'), split_axis=3, concat_axis=1, til...  6.21 us
    all_to_all x1, waiting for transfers between devices, on_device(): lax.all_to_all(d_cross_t, 'row', split_axis=2, concat_axis=1, tiled=True)  5.39 us
    all_to_all x1, starting transfers between devices, on_device(): lax.all_to_all(back_in, 'row', split_axis=0, concat_axis=0, tiled=True)  5.35 us
  transfers between devices with their start and end apart: 9, of which 7 were waited for; matrix products, arithmetic and copies ran while one was open for 4% of the time, Pallas kernels for 0%

commit v1 on v0

--- a/solution.py
+++ b/solution.py
@@ -1,6 +1,10 @@
+import functools
+
 import jax
 import jax.numpy as jnp
 from jax import lax
+from jax.experimental import pallas as pl
+from jax.experimental.pallas import tpu as pltpu
 from jax.sharding import PartitionSpec as P
 
 epsilon = 1e-05
@@ -191,6 +195,323 @@
     )
 
 
+MESH = pl.DeviceIdType.MESH
+F32 = jnp.float32
+BF16 = jnp.bfloat16
+
+
+def gather_kernel(sizes, pair_ref, cot_ref, all_ref, send_sem, recv_sem):
+    rows, subs, pairs = sizes
+    r, x, c = lax.axis_index("row"), lax.axis_index("sub"), lax.axis_index("pair")
+    half = pair_ref.shape[0]
+
+    def slot(row, sub, pair):
+        return (row * subs + sub) * pairs + pair
+
+    def copy(owner, number, **target):
+        return pltpu.make_async_remote_copy(
+            src_ref=all_ref.at[owner],
+            dst_ref=all_ref.at[owner],
+            send_sem=send_sem.at[number],
+            recv_sem=recv_sem.at[owner],
+            device_id=target,
+            device_id_type=MESH,
+        )
+
+    me = slot(r, x, c)
+    all_ref[me, :half] = pair_ref[...]
+    all_ref[me, half:] = cot_ref[...]
+
+    row_peers = [lax.rem(r + step, rows) for step in range(1, rows)]
+    barrier = pltpu.get_barrier_semaphore()
+    for peer in row_peers:
+        pl.semaphore_signal(barrier, inc=1, device_id={"row": peer}, device_id_type=MESH)
+    pl.semaphore_signal(barrier, inc=1, device_id={"sub": 1 - x}, device_id_type=MESH)
+    pl.semaphore_signal(barrier, inc=1, device_id={"pair": 1 - c}, device_id_type=MESH)
+    pl.semaphore_wait(barrier, rows + 1)
+
+    sent = []
+
+    def send(owner, **target):
+        one = copy(owner, len(sent), **target)
+        one.start()
+        sent.append(one)
+
+    for peer in row_peers:
+        send(me, row=peer)
+    send(me, sub=1 - x)
+    send(me, pair=1 - c)
+    for peer in row_peers:
+        owner = slot(peer, x, c)
+        copy(owner, 0, row=peer).wait_recv()
+        send(owner, sub=1 - x)
+        send(owner, pair=1 - c)
+    for peer in [r] + row_peers:
+        owner = slot(peer, 1 - x, c)
+        copy(owner, 0, sub=1 - x).wait_recv()
+        send(owner, pair=1 - c)
+    for peer in [r] + row_peers:
+        for sub in (x, 1 - x):
+            copy(slot(peer, sub, 1 - c), 0, pair=1 - c).wait_recv()
+    for one in sent:
+        one.wait_send()
+
+
+def norm_rows(values):
+    row_mean = jnp.mean(values, axis=-1, keepdims=True)
+    centred = values - row_mean
+    row_var = jnp.mean(centred * centred, axis=-1, keepdims=True)
+    scale = lax.rsqrt(row_var + epsilon)
+    return centred * scale, scale
+
+
+def norm_rows_back(unit, scale, cotangent):
+    first = jnp.mean(cotangent, axis=-1, keepdims=True)
+    second = jnp.mean(cotangent * unit, axis=-1, keepdims=True)
+    return scale * (cotangent - first - unit * second)
+
+
+def sigmoid(values):
+    return 0.5 * jnp.tanh(0.5 * values) + 0.5
+
+
+def dot_nn(a, b):
+    return lax.dot_general(a, b, (((1,), (0,)), ((), ())), preferred_element_type=F32)
+
+
+def dot_nt(a, b):
+    return lax.dot_general(a, b, (((1,), (1,)), ((), ())), preferred_element_type=F32)
+
+
+def dot_tn(a, b):
+    return lax.dot_general(a, b, (((0,), (0,)), ((), ())), preferred_element_type=F32)
+
+
+def triangle(out, entry, table, length, block=4):
+    def step(at, carry):
+        totals = [None] * block
+        for s in range(length):
+            rows = table[s]
+            for q in range(block):
+                term = entry(at * block + q, s) * rows
+                totals[q] = term if s == 0 else totals[q] + term
+        for q in range(block):
+            out[at * block + q] = totals[q]
+        return carry
+
+    lax.fori_loop(0, length // block, step, 0)
+
+
+def crop_kernel(
+    sizes, row_block, col_block,
+    mask_ref, all_ref, w_proj_ref, w_gate_ref, w_out_ref, pair_own_ref,
+    turned_ref, d_pair_ref, g_proj_ref, g_gate_ref, g_out_ref,
+    mask, pair, gate, left, right, right_flat, right_by_k, cot_flat, d_up, crossed,
+    d_cross, d_left, d_right, d_gate, up_flat, l_one, l_two, r_one, r_two,
+    normed, d_proj, d_gate_b,
+):
+    rows, subs, pairs = sizes
+    col_groups = subs * pairs
+    length = rows * row_block
+    half = row_block * col_block
+    band = row_block * length
+    r = lax.axis_index("row")
+    cg = lax.axis_index("sub") * pairs + lax.axis_index("pair")
+    width = w_gate_ref.shape[0]
+
+    def get(ref, at):
+        return jnp.concatenate(
+            [
+                ref[pl.ds(at * row_block, row_block), g * col_block : (g + 1) * col_block].reshape(half, width)
+                for g in range(col_groups)
+            ],
+            axis=0,
+        )
+
+    def put(ref, at, values):
+        for g in range(col_groups):
+            ref[pl.ds(at * row_block, row_block), g * col_block : (g + 1) * col_block] = values[
+                g * half : (g + 1) * half
+            ].reshape(row_block, col_block, width)
+
+    place = lax.broadcasted_iota(jnp.int32, (length, width), 0)
+    col_mask = jnp.zeros((length, width), F32)
+    for i in range(length):
+        col_mask = jnp.where(place == i, mask_ref[i].astype(F32), col_mask)
+    for i in range(length):
+        mask[i] = col_mask * mask_ref[i].astype(F32)
+
+    def front(at, carry):
+        rows_at = pl.ds(pl.multiple_of(at * band, band), band)
+        held = all_ref[pl.ds(at * col_groups, col_groups)]
+        x = held[:, :half].reshape(band, width).astype(F32)
+        cot_flat[rows_at] = held[:, half:].reshape(band, width).astype(F32)
+        put(pair, at, x)
+        unit, _ = norm_rows(x)
+        unit_b = unit.astype(BF16)
+        normed[rows_at] = unit_b
+        m = get(mask, at)
+        put(gate, at, sigmoid(dot_nn(unit_b, w_gate_ref[...])))
+        projected = dot_nn(unit_b, w_proj_ref[...])
+        for base, ref, one, two in ((0, left, l_one, l_two), (2, right, r_one, r_two)):
+            s = sigmoid(projected[:, base * width : (base + 1) * width])
+            v = projected[:, (base + 1) * width : (base + 2) * width]
+            sm = s * m
+            vs = v * sm
+            one[rows_at] = sm
+            two[rows_at] = vs * (1.0 - s)
+            put(ref, at, vs.astype(BF16).astype(F32))
+        return carry
+
+    lax.fori_loop(0, rows, front, 0)
+
+    def spread(i, carry):
+        right_flat[pl.ds(pl.multiple_of(i * length, length), length)] = right[i]
+        return carry
+
+    lax.fori_loop(0, length, spread, 0)
+    for i in range(length):
+        right_by_k[i] = right_flat[pl.ds(i, length, stride=length)]
+        d_up[i] = cot_flat[pl.ds(i, length, stride=length)]
+
+    triangle(crossed, lambda a, s: left[a, pl.ds(s, 1)], right_by_k, length)
+
+    g_out_ref[...] = jnp.zeros_like(g_out_ref)
+    g_proj_ref[...] = jnp.zeros_like(g_proj_ref)
+    g_gate_ref[...] = jnp.zeros_like(g_gate_ref)
+
+    def middle(at, carry):
+        here = pl.ds(at * row_block, row_block)
+
+        def flat(ref):
+            return ref[here].reshape(band, width)
+
+        unit, scale = norm_rows(flat(crossed).astype(BF16).astype(F32))
+        unit_b = unit.astype(BF16)
+        w_out = w_out_ref[...]
+        out_proj = dot_nn(unit_b, w_out)
+        g = flat(gate)
+        up = flat(d_up)
+        gated = g * out_proj
+        up_flat[pl.ds(pl.multiple_of(at * band, band), band)] = flat(pair) + gated
+        d_out_b = (g * up).astype(BF16)
+        d_gate[here] = (gated * up * (1.0 - g)).reshape(row_block, length, width)
+        d_unit = dot_nt(d_out_b, w_out)
+        back = norm_rows_back(unit, scale, d_unit)
+        d_cross[here] = back.astype(BF16).astype(F32).reshape(row_block, length, width)
+        g_out_ref[...] += dot_tn(unit_b, d_out_b)
+        return carry
+
+    lax.fori_loop(0, rows, middle, 0)
+
+    triangle(d_left, lambda a, s: d_cross[a, pl.ds(s, 1)], right, length)
+    triangle(d_right, lambda a, s: d_cross[s, pl.ds(a, 1)], left, length)
+
+    def finish(at, carry):
+        rows_at = pl.ds(pl.multiple_of(at * band, band), band)
+        dl, dr = get(d_left, at), get(d_right, at)
+        parts = (dl * l_two[rows_at], dl * l_one[rows_at], dr * r_two[rows_at], dr * r_one[rows_at])
+        unit_b = normed[rows_at]
+        for q, part in enumerate(parts):
+            part_b = part.astype(BF16)
+            d_proj[rows_at, q * width : (q + 1) * width] = part_b
+        g_proj_ref[...] += dot_tn(unit_b, d_proj[rows_at])
+        gate_b = get(d_gate, at).astype(BF16)
+        d_gate_b[rows_at] = gate_b
+        g_gate_ref[...] += dot_tn(unit_b, gate_b)
+        return carry
+
+    lax.fori_loop(0, rows, finish, 0)
+
+    share = 1.0 / length
+    g_proj_ref[...] = g_proj_ref[...] * share
+    g_gate_ref[...] = g_gate_ref[...] * share
+    g_out_ref[...] = g_out_ref[...] * share
+
+    own = r * col_groups + cg
+    own_rows = pl.ds(pl.multiple_of(own * half, half), half)
+    d_normed = dot_nt(d_proj[own_rows], w_proj_ref[...]) + dot_nt(d_gate_b[own_rows], w_gate_ref[...])
+    unit, scale = norm_rows(pair_own_ref[...].astype(F32))
+    up = d_up[
+        pl.ds(r * row_block, row_block), pl.ds(pl.multiple_of(cg * col_block, col_block), col_block)
+    ].reshape(half, width)
+    d_pair_ref[...] = (up + norm_rows_back(unit, scale, d_normed)).astype(BF16)
+
+    turned_rows = half // length
+    for q in range(turned_rows):
+        turned_ref[q * length : (q + 1) * length] = up_flat[
+            pl.ds(own * turned_rows + q, length, stride=length)
+        ].astype(BF16)
+
+
+def on_device_whole(sizes, pair_act, residue_mask, w_proj, w_gate, w_out, d_transposed):
+    row_block, col_block, channels = pair_act.shape
+    rows, subs, pairs = sizes
+    devices = rows * subs * pairs
+    length = rows * row_block
+    half = row_block * col_block
+    pair_own = pair_act.reshape(half, channels)
+    cot_own = d_transposed.reshape(half, channels)
+    in_vmem = pl.BlockSpec(memory_space=pltpu.VMEM)
+    everything = pl.pallas_call(
+        functools.partial(gather_kernel, sizes),
+        out_shape=jax.ShapeDtypeStruct((devices, 2 * half, channels), BF16),
+        in_specs=[in_vmem] * 2,
+        out_specs=in_vmem,
+        scratch_shapes=[
+            pltpu.SemaphoreType.DMA((devices,)),
+            pltpu.SemaphoreType.DMA((devices,)),
+        ],
+        compiler_params=pltpu.CompilerParams(collective_id=0, has_side_effects=True),
+        name="gather",
+    )(pair_own, cot_own)
+    cube = pltpu.VMEM((length, length, channels), F32)
+    flat = pltpu.VMEM((length * length, channels), F32)
+    turned, d_pair, g_proj, g_gate, g_out = pl.pallas_call(
+        functools.partial(crop_kernel, sizes, row_block, col_block),
+        out_shape=(
+            jax.ShapeDtypeStruct((half, channels), BF16),
+            jax.ShapeDtypeStruct((half, channels), BF16),
+            jax.ShapeDtypeStruct(w_proj.shape, F32),
+            jax.ShapeDtypeStruct(w_gate.shape, F32),
+            jax.ShapeDtypeStruct(w_out.shape, F32),
+        ),
+        in_specs=[pl.BlockSpec(memory_space=pltpu.SMEM)] + [in_vmem] * 5,
+        out_specs=[in_vmem] * 5,
+        scratch_shapes=[
+            cube, cube, cube, cube, cube, flat, cube, flat, cube, cube,
+            cube, cube, cube, cube, flat, flat, flat, flat, flat,
+            pltpu.VMEM((length * length, channels), BF16),
+            pltpu.VMEM((length * length, w_proj.shape[1]), BF16),
+            pltpu.VMEM((length * length, channels), BF16),
+        ],
+        compiler_params=pltpu.CompilerParams(vmem_limit_bytes=40 * 1024 * 1024),
+        name="crop",
+    )(residue_mask, everything, w_proj, w_gate, w_out, pair_own)
+    return (
+        turned.reshape(d_transposed.shape),
+        d_pair.reshape(pair_act.shape),
+        g_proj,
+        g_gate,
+        g_out,
+    )
+
+
+def choose(sizes, pair_act, residue_mask, w_proj, w_gate, w_out, d_transposed):
+    row_block, col_block, channels = pair_act.shape
+    length = sizes[0] * row_block
+    fits = (
+        length <= 32
+        and row_block % 8 == 0
+        and col_block % 8 == 0
+        and sizes[1:] == (2, 2)
+        and w_out.shape == (128, 128)
+        and w_proj.shape == (128, 512)
+    )
+    body = functools.partial(on_device_whole, sizes) if fits else on_device
+    return body(pair_act, residue_mask, w_proj, w_gate, w_out, d_transposed)
+
+
 def solution(mesh):
     in_specs = (
         P(("crops", "row"), ("sub", "pair"), None),
@@ -207,6 +528,7 @@
         P("crops", None),
         P("crops", None),
     )
+    sizes = (mesh.shape["row"], mesh.shape["sub"], mesh.shape["pair"])
     return jax.shard_map(
-        on_device, mesh=mesh, in_specs=in_specs, out_specs=out_specs, check_vma=False
-    )
+        functools.partial(choose, sizes), mesh=mesh, in_specs=in_specs, out_specs=out_specs, check_vma=False
+    )

time: 207 us -> 27.9 us (0.13)
  waiting for transfers between devices: 108 us -> 0 us
  blocking collectives: 32.7 us -> 0 us
  starting transfers between devices: 29.9 us -> 0 us
  Pallas kernels: 0 us -> 25.8 us
  between operations: 14.4 us -> 0.73 us
  local copies, waits for them, and re-layouts: 10.9 us -> 1.06 us
  other arithmetic: 5.28 us -> 0 us
  matrix products: 4.67 us -> 0 us
    psum x1 -> x0, waiting for transfers between devices: 88 us -> none  [on_device(): lax.psum((weight_terms[0], weight_terms[1], weight_terms[2]), ('row', 'su...]
    all_to_all x8 -> x0, starting transfers between devices: 29.8 us -> none  [the longest x2 7.59 us: to_channels(): lax.all_to_all(sectioning, ('sub', 'pair'), split_axis=2, concat_axis=0,...]
    all_gather x2 -> x0, blocking collectives: 26.5 us -> none  [the longest x1 13.5 us: on_device(): lax.all_gather(right_t, 'row', axis=1, tiled=True)]
    pallas_call x0 -> x2, Pallas kernels: none -> 25.8 us  [the longest x1 15 us: on_device_whole(): pl.pallas_call(functools.partial(gather_kernel, sizes), out_shape=jax.Sha...]
    all_to_all x8 -> x0, waiting for transfers between devices: 20.2 us -> none  [the longest x1 5.39 us: on_device(): lax.all_to_all(d_cross_t, 'row', split_axis=2, concat_axis=1, tiled=True)]
    all_to_all x1 -> x0, blocking collectives: 6.21 us -> none  [from_channels(): lax.all_to_all(stacked, ('sub', 'pair'), split_axis=3, concat_axis=1, til...]
    unnamed x27 -> x12, local copies, waits for them, and re-layouts: 6.74 us -> 1.06 us
    dot_general x12 -> x0, matrix products: 4.67 us -> none  [the longest x1 1 us: on_device(): jnp.einsum('rc,rd->cd', normed, d_proj, preferred_element_type=jnp.float32)]
  transfers between devices with their start and end apart: 9 -> 0, of which waited for: 7 -> 0; matrix products, arithmetic and copies ran while one was open for 4% -> 0% of each run, Pallas kernels for 0% -> 0%
where the time goes in v1:
time: 27.9 us; the launch traced here: 27.6 us
  Pallas kernels  25.8 us (92%)
  local copies, waits for them, and re-layouts  1.06 us (4%)
  between operations  0.73 us (3%)
    pallas_call x1, Pallas kernels, on_device_whole(): pl.pallas_call(functools.partial(gather_kernel, sizes), out_shape=jax.Sha...  15 us
    pallas_call x1, Pallas kernels, on_device_whole(): pl.pallas_call(functools.partial(crop_kernel, sizes, row_block, col_block...  10.9 us
    unnamed x12, local copies, waits for them, and re-layouts  1.06 us

profile of v1, /device:TPU:0, one launch (start us, length us, event | category | flops | bytes accessed | tf_op | source)
XLA Modules:
  0.0 27.6 jit_solution(18111745516078192652)
XLA Ops:
  0.6 0.0 copy-start.1
  0.6 0.0 copy-start.2
  0.7 0.0 copy-start.3
  0.7 0.0 copy-start.4
  0.7 0.0 copy-start.5
  0.7 15.0 %gather.1.all_ref = bf16[16,128,128]{2,1,0:T(8,128)(2,1)} custom-call(bf16[64,128]{1,0:T(8,128)(2,1)} %bitcast.4, bf16[64,128]{1,0:T(8,128)(2,1)} %bitcast.6), custom_call_target="tpu_custom_call" | custom-call | tf_op jit(solution)/shard_map/gather/pallas_call | solution.py:456
  15.6 0.0 copy-done.1
  15.7 0.0 copy-done.2
  15.7 0.0 copy-done.3
  15.7 0.0 copy-done.4
  15.7 0.0 copy-done.5
  15.7 0.0 copy-start
  15.7 1.0 %copy-done = bf16[16,128,128]{2,1,0:T(8,128)(2,1)S(1)} copy-done((bf16[16,128,128]{2,1,0:T(8,128)(2,1)S(1)}, bf16[16,128,128]{2,1,0:T(8,128)(2,1)}, u32[]{:S(2)}) %copy-start) | copy-done | bytes 524312
  16.7 10.9 %crop.1 = (bf16[64,128]{1,0:T(8,128)(2,1)}, bf16[64,128]{1,0:T(8,128)(2,1)}, f32[128,512]{1,0:T(8,128)}, f32[128,128]{1,0:T(8,128)}, f32[128,128]{1,0:T(8,128)}) custom-call(s32[32]{0:T(128)S(1)} %copy-done.5, bf16[16,128,128]{2,1,0:T(8,128)(2,1)S(1)} %copy-done, bf16[128,512]{1,0:T(8,128)(2,1)S(1)} %copy-done.1, bf16[128,128]{1,0:T(8,128)(2,1)S(1)} %copy-done.3, ...), custom_call_target="tpu_custom_call" | custom-call | tf_op jit(solution)/shard_map/crop/pallas_call | solution.py:470
Async XLA Ops:
  0.6 15.0 %copy-start.1 = (bf16[128,512]{1,0:T(8,128)(2,1)S(1)}, bf16[128,512]{1,0:T(8,128)(2,1)}, u32[]{:S(2)}) copy-start(bf16[128,512]{1,0:T(8,128)(2,1)} %w_proj_ref.1) | copy-start | bytes 393220
  0.6 15.0 %copy-start.2 = (bf16[8,8,128]{2,1,0:T(8,128)(2,1)S(1)}, bf16[8,8,128]{2,1,0:T(8,128)(2,1)}, u32[]{:S(2)}) copy-start(bf16[8,8,128]{2,1,0:T(8,128)(2,1)} %param.6) | copy-start | bytes 49156
  0.7 15.0 %copy-start.3 = (bf16[128,128]{1,0:T(8,128)(2,1)S(1)}, bf16[128,128]{1,0:T(8,128)(2,1)}, u32[]{:S(2)}) copy-start(bf16[128,128]{1,0:T(8,128)(2,1)} %w_gate_ref.1) | copy-start | bytes 98308
  0.7 15.0 %copy-start.4 = (bf16[128,128]{1,0:T(8,128)(2,1)S(1)}, bf16[128,128]{1,0:T(8,128)(2,1)}, u32[]{:S(2)}) copy-start(bf16[128,128]{1,0:T(8,128)(2,1)} %w_out_ref.1) | copy-start | bytes 98308
  0.7 15.0 %copy-start.5 = (s32[32]{0:T(128)S(1)}, s32[32]{0:T(128)}, u32[]{:S(2)}) copy-start(s32[32]{0:T(128)} %mask_ref.1) | copy-start | bytes 388
  15.7 1.0 %copy-start = (bf16[16,128,128]{2,1,0:T(8,128)(2,1)S(1)}, bf16[16,128,128]{2,1,0:T(8,128)(2,1)}, u32[]{:S(2)}) copy-start(bf16[16,128,128]{2,1,0:T(8,128)(2,1)} %gather.1.all_ref) | copy-start | bytes 1572868

commit v2 on v1

--- a/solution.py
+++ b/solution.py
@@ -200,63 +200,6 @@
 BF16 = jnp.bfloat16
 
 
-def gather_kernel(sizes, pair_ref, cot_ref, all_ref, send_sem, recv_sem):
-    rows, subs, pairs = sizes
-    r, x, c = lax.axis_index("row"), lax.axis_index("sub"), lax.axis_index("pair")
-    half = pair_ref.shape[0]
-
-    def slot(row, sub, pair):
-        return (row * subs + sub) * pairs + pair
-
-    def copy(owner, number, **target):
-        return pltpu.make_async_remote_copy(
-            src_ref=all_ref.at[owner],
-            dst_ref=all_ref.at[owner],
-            send_sem=send_sem.at[number],
-            recv_sem=recv_sem.at[owner],
-            device_id=target,
-            device_id_type=MESH,
-        )
-
-    me = slot(r, x, c)
-    all_ref[me, :half] = pair_ref[...]
-    all_ref[me, half:] = cot_ref[...]
-
-    row_peers = [lax.rem(r + step, rows) for step in range(1, rows)]
-    barrier = pltpu.get_barrier_semaphore()
-    for peer in row_peers:
-        pl.semaphore_signal(barrier, inc=1, device_id={"row": peer}, device_id_type=MESH)
-    pl.semaphore_signal(barrier, inc=1, device_id={"sub": 1 - x}, device_id_type=MESH)
-    pl.semaphore_signal(barrier, inc=1, device_id={"pair": 1 - c}, device_id_type=MESH)
-    pl.semaphore_wait(barrier, rows + 1)
-
-    sent = []
-
-    def send(owner, **target):
-        one = copy(owner, len(sent), **target)
-        one.start()
-        sent.append(one)
-
-    for peer in row_peers:
-        send(me, row=peer)
-    send(me, sub=1 - x)
-    send(me, pair=1 - c)
-    for peer in row_peers:
-        owner = slot(peer, x, c)
-        copy(owner, 0, row=peer).wait_recv()
-        send(owner, sub=1 - x)
-        send(owner, pair=1 - c)
-    for peer in [r] + row_peers:
-        owner = slot(peer, 1 - x, c)
-        copy(owner, 0, sub=1 - x).wait_recv()
-        send(owner, pair=1 - c)
-    for peer in [r] + row_peers:
-        for sub in (x, 1 - x):
-            copy(slot(peer, sub, 1 - c), 0, pair=1 - c).wait_recv()
-    for one in sent:
-        one.wait_send()
-
-
 def norm_rows(values):
     row_mean = jnp.mean(values, axis=-1, keepdims=True)
     centred = values - row_mean
@@ -302,57 +245,124 @@
     lax.fori_loop(0, length // block, step, 0)
 
 
-def crop_kernel(
-    sizes, row_block, col_block,
-    mask_ref, all_ref, w_proj_ref, w_gate_ref, w_out_ref, pair_own_ref,
-    turned_ref, d_pair_ref, g_proj_ref, g_gate_ref, g_out_ref,
-    mask, pair, gate, left, right, right_flat, right_by_k, cot_flat, d_up, crossed,
-    d_cross, d_left, d_right, d_gate, up_flat, l_one, l_two, r_one, r_two,
-    normed, d_proj, d_gate_b,
+def get(ref, at, sizes, shape):
+    row_block, col_block, width = shape
+    return jnp.concatenate(
+        [
+            ref[pl.ds(at * row_block, row_block), g * col_block : (g + 1) * col_block].reshape(
+                row_block * col_block, width
+            )
+            for g in range(sizes[1] * sizes[2])
+        ],
+        axis=0,
+    )
+
+
+def put(ref, at, sizes, shape, values):
+    row_block, col_block, width = shape
+    half = row_block * col_block
+    for g in range(sizes[1] * sizes[2]):
+        ref[pl.ds(at * row_block, row_block), g * col_block : (g + 1) * col_block] = values[
+            g * half : (g + 1) * half
+        ].reshape(row_block, col_block, width)
+
+
+def front_kernel(
+    sizes, shape,
+    pair_hbm, cot_hbm, mask_hbm, w_proj_hbm, w_gate_hbm,
+    cot_all, pair, gate, left, right, l_one, l_two, r_one, r_two, normed,
+    pair_all, w_proj, w_gate, mask_row, mask, own_sem, send_sem, recv_sem,
 ):
     rows, subs, pairs = sizes
+    row_block, col_block, width = shape
     col_groups = subs * pairs
     length = rows * row_block
     half = row_block * col_block
     band = row_block * length
-    r = lax.axis_index("row")
-    cg = lax.axis_index("sub") * pairs + lax.axis_index("pair")
-    width = w_gate_ref.shape[0]
-
-    def get(ref, at):
-        return jnp.concatenate(
-            [
-                ref[pl.ds(at * row_block, row_block), g * col_block : (g + 1) * col_block].reshape(half, width)
-                for g in range(col_groups)
-            ],
-            axis=0,
-        )
-
-    def put(ref, at, values):
-        for g in range(col_groups):
-            ref[pl.ds(at * row_block, row_block), g * col_block : (g + 1) * col_block] = values[
-                g * half : (g + 1) * half
-            ].reshape(row_block, col_block, width)
-
+    r, x, c = lax.axis_index("row"), lax.axis_index("sub"), lax.axis_index("pair")
+
+    def slot(row, sub, pair_at):
+        return (row * subs + sub) * pairs + pair_at
+
+    me = slot(r, x, c)
+    if rows == 4:
+        order = [r, r + 1 - 2 * (r % 2), r + 2 - 4 * (r // 2), 3 - r]
+    else:
+        order = [(r + step) % rows for step in range(rows)]
+    far_first = [(order[q], sub) for q in reversed(range(1, rows)) for sub in (1 - x, x)] + [(r, 1 - x)]
+
+    local = [
+        pltpu.make_async_copy(pair_hbm, pair_all.at[me], own_sem.at[0]),
+        pltpu.make_async_copy(cot_hbm, cot_all.at[me], own_sem.at[1]),
+        pltpu.make_async_copy(mask_hbm, mask_row, own_sem.at[2]),
+        pltpu.make_async_copy(w_proj_hbm, w_proj, own_sem.at[3]),
+        pltpu.make_async_copy(w_gate_hbm, w_gate, own_sem.at[4]),
+    ]
+    for one in local:
+        one.start()
+
+    barrier = pltpu.get_barrier_semaphore()
+    for row, sub in far_first:
+        pl.semaphore_signal(barrier, inc=1, device_id={"row": row, "sub": sub}, device_id_type=MESH)
+    pl.semaphore_signal(barrier, inc=1, device_id={"pair": 1 - c}, device_id_type=MESH)
+
+    local[2].wait()
     place = lax.broadcasted_iota(jnp.int32, (length, width), 0)
     col_mask = jnp.zeros((length, width), F32)
     for i in range(length):
-        col_mask = jnp.where(place == i, mask_ref[i].astype(F32), col_mask)
+        col_mask = jnp.where(place == i, mask_row[i].astype(F32), col_mask)
     for i in range(length):
-        mask[i] = col_mask * mask_ref[i].astype(F32)
-
-    def front(at, carry):
+        mask[i] = col_mask * mask_row[i].astype(F32)
+    for one in (local[0], local[1], local[3], local[4]):
+        one.wait()
+    pl.semaphore_wait(barrier, len(far_first) + 1)
+
+    buffers = (pair_all, cot_all)
+    sent = ([], [])
+
+    def copy(kind, owner, number, target):
+        return pltpu.make_async_remote_copy(
+            src_ref=buffers[kind].at[owner],
+            dst_ref=buffers[kind].at[owner],
+            send_sem=send_sem.at[kind, number],
+            recv_sem=recv_sem.at[kind, owner],
+            device_id=target,
+            device_id_type=MESH,
+        )
+
+    def send(kind, owner, target):
+        one = copy(kind, owner, len(sent[kind]), target)
+        one.start()
+        sent[kind].append(one)
+
+    other = {"pair": 1 - c}
+
+    def send_own(kind):
+        for row, sub in far_first:
+            send(kind, me, {"row": row, "sub": sub})
+        send(kind, me, other)
+
+    def pass_on(kind, q):
+        for sub in (1 - x,) if q == 0 else (x, 1 - x):
+            owner = slot(order[q], sub, c)
+            copy(kind, owner, 0, other).wait_recv()
+            send(kind, owner, other)
+
+    def from_other(kind, q):
+        for sub in (x, 1 - x):
+            copy(kind, slot(order[q], sub, 1 - c), 0, other).wait_recv()
+
+    def front(q):
+        at = order[q]
         rows_at = pl.ds(pl.multiple_of(at * band, band), band)
-        held = all_ref[pl.ds(at * col_groups, col_groups)]
-        x = held[:, :half].reshape(band, width).astype(F32)
-        cot_flat[rows_at] = held[:, half:].reshape(band, width).astype(F32)
-        put(pair, at, x)
-        unit, _ = norm_rows(x)
+        values = pair_all[pl.ds(at * col_groups, col_groups)].reshape(band, width).astype(F32)
+        put(pair, at, sizes, shape, values)
+        unit, _ = norm_rows(values)
         unit_b = unit.astype(BF16)
         normed[rows_at] = unit_b
-        m = get(mask, at)
-        put(gate, at, sigmoid(dot_nn(unit_b, w_gate_ref[...])))
-        projected = dot_nn(unit_b, w_proj_ref[...])
+        m = get(mask, at, sizes, shape)
+        put(gate, at, sizes, shape, sigmoid(dot_nn(unit_b, w_gate[...])))
+        projected = dot_nn(unit_b, w_proj[...])
         for base, ref, one, two in ((0, left, l_one, l_two), (2, right, r_one, r_two)):
             s = sigmoid(projected[:, base * width : (base + 1) * width])
             v = projected[:, (base + 1) * width : (base + 2) * width]
@@ -360,16 +370,47 @@
             vs = v * sm
             one[rows_at] = sm
             two[rows_at] = vs * (1.0 - s)
-            put(ref, at, vs.astype(BF16).astype(F32))
-        return carry
-
-    lax.fori_loop(0, rows, front, 0)
-
-    def spread(i, carry):
-        right_flat[pl.ds(pl.multiple_of(i * length, length), length)] = right[i]
-        return carry
-
-    lax.fori_loop(0, length, spread, 0)
+            put(ref, at, sizes, shape, vs.astype(BF16).astype(F32))
+
+    send_own(0)
+    send_own(1)
+    pass_on(0, 0)
+    pass_on(0, 1)
+    from_other(0, 0)
+    front(0)
+    for q in range(2, rows):
+        pass_on(0, q)
+    pass_on(1, 0)
+    for q in range(1, rows):
+        from_other(0, q)
+        front(q)
+        pass_on(1, q)
+    for q in range(rows):
+        from_other(1, q)
+    for kind in (0, 1):
+        for one in sent[kind]:
+            one.wait_send()
+
+
+def crop_kernel(
+    sizes, shape,
+    cot_all, pair, gate, left, right, l_one, l_two, r_one, r_two, normed,
+    w_proj_ref, w_gate_ref, w_out_ref, pair_own_ref,
+    turned_ref, d_pair_ref, g_proj_ref, g_gate_ref, g_out_ref,
+    right_by_k, cot_flat, d_up, crossed,
+    d_cross, d_left, d_right, d_gate, up_flat, d_proj, d_gate_b,
+):
+    rows, subs, pairs = sizes
+    row_block, col_block, width = shape
+    col_groups = subs * pairs
+    length = rows * row_block
+    half = row_block * col_block
+    band = row_block * length
+    r = lax.axis_index("row")
+    cg = lax.axis_index("sub") * pairs + lax.axis_index("pair")
+
+    cot_flat[...] = cot_all[...].reshape(length * length, width).astype(F32)
+    right_flat = right.reshape(length * length, width)
     for i in range(length):
         right_by_k[i] = right_flat[pl.ds(i, length, stride=length)]
         d_up[i] = cot_flat[pl.ds(i, length, stride=length)]
@@ -409,14 +450,14 @@
 
     def finish(at, carry):
         rows_at = pl.ds(pl.multiple_of(at * band, band), band)
-        dl, dr = get(d_left, at), get(d_right, at)
+        dl, dr = get(d_left, at, sizes, shape), get(d_right, at, sizes, shape)
         parts = (dl * l_two[rows_at], dl * l_one[rows_at], dr * r_two[rows_at], dr * r_one[rows_at])
         unit_b = normed[rows_at]
         for q, part in enumerate(parts):
             part_b = part.astype(BF16)
             d_proj[rows_at, q * width : (q + 1) * width] = part_b
         g_proj_ref[...] += dot_tn(unit_b, d_proj[rows_at])
-        gate_b = get(d_gate, at).astype(BF16)
+        gate_b = get(d_gate, at, sizes, shape).astype(BF16)
         d_gate_b[rows_at] = gate_b
         g_gate_ref[...] += dot_tn(unit_b, gate_b)
         return carry
@@ -452,23 +493,40 @@
     half = row_block * col_block
     pair_own = pair_act.reshape(half, channels)
     cot_own = d_transposed.reshape(half, channels)
+    shape = (row_block, col_block, channels)
     in_vmem = pl.BlockSpec(memory_space=pltpu.VMEM)
-    everything = pl.pallas_call(
-        functools.partial(gather_kernel, sizes),
-        out_shape=jax.ShapeDtypeStruct((devices, 2 * half, channels), BF16),
-        in_specs=[in_vmem] * 2,
-        out_specs=in_vmem,
+    in_hbm = pl.BlockSpec(memory_space=pltpu.HBM)
+    cube = (length, length, channels)
+    flat = (length * length, channels)
+    kept = [jax.ShapeDtypeStruct(cube, F32)] * 4 + [jax.ShapeDtypeStruct(flat, F32)] * 4
+    held = pl.pallas_call(
+        functools.partial(front_kernel, sizes, shape),
+        out_shape=[
+            jax.ShapeDtypeStruct((devices, half, channels), BF16),
+            *kept,
+            jax.ShapeDtypeStruct(flat, BF16),
+        ],
+        in_specs=[in_hbm] * 5,
+        out_specs=[in_vmem] * 10,
         scratch_shapes=[
-            pltpu.SemaphoreType.DMA((devices,)),
-            pltpu.SemaphoreType.DMA((devices,)),
+            pltpu.VMEM((devices, half, channels), BF16),
+            pltpu.VMEM(w_proj.shape, BF16),
+            pltpu.VMEM(w_gate.shape, BF16),
+            pltpu.SMEM((length,), jnp.int32),
+            pltpu.VMEM(cube, F32),
+            pltpu.SemaphoreType.DMA((5,)),
+            pltpu.SemaphoreType.DMA((2, devices)),
+            pltpu.SemaphoreType.DMA((2, devices)),
         ],
-        compiler_params=pltpu.CompilerParams(collective_id=0, has_side_effects=True),
-        name="gather",
-    )(pair_own, cot_own)
-    cube = pltpu.VMEM((length, length, channels), F32)
-    flat = pltpu.VMEM((length * length, channels), F32)
+        compiler_params=pltpu.CompilerParams(
+            collective_id=0, has_side_effects=True, vmem_limit_bytes=16 * 1024 * 1024
+        ),
+        name="front",
+    )(pair_own, cot_own, residue_mask, w_proj, w_gate)
+    cube_room = pltpu.VMEM(cube, F32)
+    flat_room = pltpu.VMEM(flat, F32)
     turned, d_pair, g_proj, g_gate, g_out = pl.pallas_call(
-        functools.partial(crop_kernel, sizes, row_block, col_block),
+        functools.partial(crop_kernel, sizes, shape),
         out_shape=(
             jax.ShapeDtypeStruct((half, channels), BF16),
             jax.ShapeDtypeStruct((half, channels), BF16),
@@ -476,18 +534,17 @@
             jax.ShapeDtypeStruct(w_gate.shape, F32),
             jax.ShapeDtypeStruct(w_out.shape, F32),
         ),
-        in_specs=[pl.BlockSpec(memory_space=pltpu.SMEM)] + [in_vmem] * 5,
+        in_specs=[in_vmem] * 14,
         out_specs=[in_vmem] * 5,
         scratch_shapes=[
-            cube, cube, cube, cube, cube, flat, cube, flat, cube, cube,
-            cube, cube, cube, cube, flat, flat, flat, flat, flat,
-            pltpu.VMEM((length * length, channels), BF16),
+            cube_room, flat_room, cube_room, cube_room,
+            cube_room, cube_room, cube_room, cube_room, flat_room,
             pltpu.VMEM((length * length, w_proj.shape[1]), BF16),
-            pltpu.VMEM((length * length, channels), BF16),
+            pltpu.VMEM(flat, BF16),
         ],
-        compiler_params=pltpu.CompilerParams(vmem_limit_bytes=40 * 1024 * 1024),
+        compiler_params=pltpu.CompilerParams(vmem_limit_bytes=24 * 1024 * 1024),
         name="crop",
-    )(residue_mask, everything, w_proj, w_gate, w_out, pair_own)
+    )(*held, w_proj, w_gate, w_out, pair_own)
     return (
         turned.reshape(d_transposed.shape),
         d_pair.reshape(pair_act.shape),

time: 27.9 us -> 29.2 us (1.047)
  local copies, waits for them, and re-layouts: 1.06 us -> 4.44 us
  Pallas kernels: 25.8 us -> 23.7 us
    unnamed x12 -> x16, local copies, waits for them, and re-layouts: 1.06 us -> 4.44 us
    pallas_call x2, Pallas kernels: 25.8 us -> 23.7 us  [the longest x1 15.2 us: on_device_whole(): pl.pallas_call(functools.partial(front_kernel, sizes, shape), out_shape=[...]
where the time goes in v2:
time: 29.2 us; the launch traced here: 28.8 us
  Pallas kernels  23.7 us (81%)
  local copies, waits for them, and re-layouts  4.44 us (15%)
  between operations  0.68 us (2%)
    pallas_call x1, Pallas kernels, on_device_whole(): pl.pallas_call(functools.partial(front_kernel, sizes, shape), out_shape=[...  15.2 us
    pallas_call x1, Pallas kernels, on_device_whole(): pl.pallas_call(functools.partial(crop_kernel, sizes, shape), out_shape=(j...  8.48 us
    unnamed x16, local copies, waits for them, and re-layouts  4.44 us

profile of v2, /device:TPU:0, one launch (start us, length us, event | category | flops | bytes accessed | tf_op | source)
XLA Modules:
  0.0 28.8 jit_solution(17912148921331682503)
XLA Ops:
  0.6 0.0 copy-start.7
  0.6 0.6 %copy-done.7 = s32[32]{0:T(128)S(1)} copy-done((s32[32]{0:T(128)S(1)}, s32[32]{0:T(128)}, u32[]{:S(2)}) %copy-start.7) | copy-done | bytes 152
  1.3 0.0 copy-start
  1.3 0.9 %copy-done = bf16[128,512]{1,0:T(8,128)(2,1)S(1)} copy-done((bf16[128,512]{1,0:T(8,128)(2,1)S(1)}, bf16[128,512]{1,0:T(8,128)(2,1)}, u32[]{:S(2)}) %copy-start) | copy-done | bytes 131096
  2.2 0.0 copy-start.2
  2.2 0.8 %copy-done.2 = bf16[128,128]{1,0:T(8,128)(2,1)S(1)} copy-done((bf16[128,128]{1,0:T(8,128)(2,1)S(1)}, bf16[128,128]{1,0:T(8,128)(2,1)}, u32[]{:S(2)}) %copy-start.2) | copy-done | bytes 32792
  3.0 0.0 copy-start.3
  3.0 0.7 %copy-done.3 = bf16[8,8,128]{2,1,0:T(8,128)(2,1)S(1)} copy-done((bf16[8,8,128]{2,1,0:T(8,128)(2,1)S(1)}, bf16[8,8,128]{2,1,0:T(8,128)(2,1)}, u32[]{:S(2)}) %copy-start.3) | copy-done | bytes 16408
  3.7 0.0 copy-start.6
  3.7 0.7 %copy-done.6 = bf16[2,32,128]{2,1,0:T(8,128)(2,1)S(1)} copy-done((bf16[2,32,128]{2,1,0:T(8,128)(2,1)S(1)}, bf16[2,32,128]{2,1,0:T(8,128)(2,1)}, u32[]{:S(2)}) %copy-start.6) | copy-done | bytes 16408
  4.4 0.0 copy-start.1
  4.4 0.0 copy-start.5
  4.4 15.2 %front.1 = (bf16[16,64,128]{2,1,0:T(8,128)(2,1)S(1)}, f32[32,32,128]{2,1,0:T(8,128)S(1)}, f32[32,32,128]{2,1,0:T(8,128)S(1)}, f32[32,32,128]{2,1,0:T(8,128)S(1)}...) custom-call(bf16[64,128]{1,0:T(8,128)(2,1)S(1)} %bitcast.4, ...), custom_call_target="tpu_custom_call" | custom-call | tf_op jit(solution)/shard_map/front/pallas_call | solution.py:502
  19.6 0.0 copy-start.4
  19.6 0.0 copy-done.1
  19.7 0.0 copy-done.5
  19.7 0.7 %copy-done.4 = bf16[8,8,128]{2,1,0:T(8,128)(2,1)S(1)} copy-done((bf16[8,8,128]{2,1,0:T(8,128)(2,1)S(1)}, bf16[8,8,128]{2,1,0:T(8,128)(2,1)}, u32[]{:S(2)}) %copy-start.4) | copy-done | bytes 16408
  20.4 8.5 %crop.1 = (bf16[64,128]{1,0:T(8,128)(2,1)}, bf16[64,128]{1,0:T(8,128)(2,1)}, f32[128,512]{1,0:T(8,128)}, f32[128,128]{1,0:T(8,128)}, f32[128,128]{1,0:T(8,128)}) custom-call(bf16[16,64,128]{2,1,0:T(8,128)(2,1)S(1)} %get-tuple-element.20.cot_all, f32[32,32,128]{2,1,0:T(8,128)S(1)} %get-tuple-element.21.pair, f32[32,32,128]{2,1,0:T(8,128)S(1)} %get-tuple-element.22.gate, ...), custom_call_target="tpu_custom_call" | custom-call | tf_op jit(solution)/shard_map/crop/pallas_call | solution.py:528
Async XLA Ops:
  0.6 0.7 %copy-start.7 = (s32[32]{0:T(128)S(1)}, s32[32]{0:T(128)}, u32[]{:S(2)}) copy-start(s32[32]{0:T(128)} %mask_hbm.1) | copy-start | bytes 388
  1.3 0.9 %copy-start = (bf16[128,512]{1,0:T(8,128)(2,1)S(1)}, bf16[128,512]{1,0:T(8,128)(2,1)}, u32[]{:S(2)}) copy-start(bf16[128,512]{1,0:T(8,128)(2,1)} %w_proj_ref.1) | copy-start | bytes 393220
  2.2 0.8 %copy-start.2 = (bf16[128,128]{1,0:T(8,128)(2,1)S(1)}, bf16[128,128]{1,0:T(8,128)(2,1)}, u32[]{:S(2)}) copy-start(bf16[128,128]{1,0:T(8,128)(2,1)} %w_gate_ref.1) | copy-start | bytes 98308
  3.0 0.7 %copy-start.3 = (bf16[8,8,128]{2,1,0:T(8,128)(2,1)S(1)}, bf16[8,8,128]{2,1,0:T(8,128)(2,1)}, u32[]{:S(2)}) copy-start(bf16[8,8,128]{2,1,0:T(8,128)(2,1)} %param.6) | copy-start | bytes 49156
  3.7 0.7 %copy-start.6 = (bf16[2,32,128]{2,1,0:T(8,128)(2,1)S(1)}, bf16[2,32,128]{2,1,0:T(8,128)(2,1)}, u32[]{:S(2)}) copy-start(bf16[2,32,128]{2,1,0:T(8,128)(2,1)} %param.11) | copy-start | bytes 49156
  4.4 15.3 %copy-start.1 = (bf16[128,512]{1,0:T(8,128)(2,1)S(1)}, bf16[128,512]{1,0:T(8,128)(2,1)}, u32[]{:S(2)}) copy-start(bf16[128,512]{1,0:T(8,128)(2,1)} %w_proj_ref.1) | copy-start | bytes 393220
  4.4 15.3 %copy-start.5 = (bf16[128,128]{1,0:T(8,128)(2,1)S(1)}, bf16[128,128]{1,0:T(8,128)(2,1)}, u32[]{:S(2)}) copy-start(bf16[128,128]{1,0:T(8,128)(2,1)} %w_out_ref.1) | copy-start | bytes 98308
  19.6 0.7 %copy-start.4 = (bf16[8,8,128]{2,1,0:T(8,128)(2,1)S(1)}, bf16[8,8,128]{2,1,0:T(8,128)(2,1)}, u32[]{:S(2)}) copy-start(bf16[8,8,128]{2,1,0:T(8,128)(2,1)} %param.6) | copy-start | bytes 49156

commit v3 on v2

--- a/solution.py
+++ b/solution.py
@@ -230,7 +230,7 @@
     return lax.dot_general(a, b, (((0,), (0,)), ((), ())), preferred_element_type=F32)
 
 
-def triangle(out, entry, table, length, block=4):
+def triangle(out, entry, table, length, block=4, first=0, last=None):
     def step(at, carry):
         totals = [None] * block
         for s in range(length):
@@ -242,7 +242,7 @@
             out[at * block + q] = totals[q]
         return carry
 
-    lax.fori_loop(0, length // block, step, 0)
+    lax.fori_loop(first, length // block if last is None else last, step, 0)
 
 
 def get(ref, at, sizes, shape):
@@ -270,8 +270,8 @@
 def front_kernel(
     sizes, shape,
     pair_hbm, cot_hbm, mask_hbm, w_proj_hbm, w_gate_hbm,
-    cot_all, pair, gate, left, right, l_one, l_two, r_one, r_two, normed,
-    pair_all, w_proj, w_gate, mask_row, mask, own_sem, send_sem, recv_sem,
+    cot_all, pair, gate, left, right, crossed, l_one, l_two, r_one, r_two, normed,
+    pair_all, right_by_k, w_proj, w_gate, mask_row, mask, own_sem, send_sem, recv_sem,
 ):
     rows, subs, pairs = sizes
     row_block, col_block, width = shape
@@ -380,11 +380,19 @@
     front(0)
     for q in range(2, rows):
         pass_on(0, q)
-    pass_on(1, 0)
     for q in range(1, rows):
         from_other(0, q)
         front(q)
+    right_flat = right.reshape(length * length, width)
+    for i in range(length):
+        right_by_k[i] = right_flat[pl.ds(i, length, stride=length)]
+    middle = length // 8
+    pass_on(1, 0)
+    pass_on(1, 1)
+    triangle(crossed, lambda a, s: left[a, pl.ds(s, 1)], right_by_k, length, last=middle)
+    for q in range(2, rows):
         pass_on(1, q)
+    triangle(crossed, lambda a, s: left[a, pl.ds(s, 1)], right_by_k, length, first=middle)
     for q in range(rows):
         from_other(1, q)
     for kind in (0, 1):
@@ -394,10 +402,10 @@
 
 def crop_kernel(
     sizes, shape,
-    cot_all, pair, gate, left, right, l_one, l_two, r_one, r_two, normed,
-    w_proj_ref, w_gate_ref, w_out_ref, pair_own_ref,
+    cot_all, pair, gate, left, right, crossed, l_one, l_two, r_one, r_two, normed,
+    w_proj_ref, w_gate_ref, w_out_ref,
     turned_ref, d_pair_ref, g_proj_ref, g_gate_ref, g_out_ref,
-    right_by_k, cot_flat, d_up, crossed,
+    cot_flat, d_up,
     d_cross, d_left, d_right, d_gate, up_flat, d_proj, d_gate_b,
 ):
     rows, subs, pairs = sizes
@@ -410,12 +418,8 @@
     cg = lax.axis_index("sub") * pairs + lax.axis_index("pair")
 
     cot_flat[...] = cot_all[...].reshape(length * length, width).astype(F32)
-    right_flat = right.reshape(length * length, width)
     for i in range(length):
-        right_by_k[i] = right_flat[pl.ds(i, length, stride=length)]
         d_up[i] = cot_flat[pl.ds(i, length, stride=length)]
-
-    triangle(crossed, lambda a, s: left[a, pl.ds(s, 1)], right_by_k, length)
 
     g_out_ref[...] = jnp.zeros_like(g_out_ref)
     g_proj_ref[...] = jnp.zeros_like(g_proj_ref)
@@ -472,10 +476,13 @@
     own = r * col_groups + cg
     own_rows = pl.ds(pl.multiple_of(own * half, half), half)
     d_normed = dot_nt(d_proj[own_rows], w_proj_ref[...]) + dot_nt(d_gate_b[own_rows], w_gate_ref[...])
-    unit, scale = norm_rows(pair_own_ref[...].astype(F32))
-    up = d_up[
-        pl.ds(r * row_block, row_block), pl.ds(pl.multiple_of(cg * col_block, col_block), col_block)
-    ].reshape(half, width)
+
+    def own_block(ref):
+        columns = pl.ds(pl.multiple_of(cg * col_block, col_block), col_block)
+        return ref[pl.ds(r * row_block, row_block), columns].reshape(half, width)
+
+    unit, scale = norm_rows(own_block(pair))
+    up = own_block(d_up)
     d_pair_ref[...] = (up + norm_rows_back(unit, scale, d_normed)).astype(BF16)
 
     turned_rows = half // length
@@ -498,7 +505,7 @@
     in_hbm = pl.BlockSpec(memory_space=pltpu.HBM)
     cube = (length, length, channels)
     flat = (length * length, channels)
-    kept = [jax.ShapeDtypeStruct(cube, F32)] * 4 + [jax.ShapeDtypeStruct(flat, F32)] * 4
+    kept = [jax.ShapeDtypeStruct(cube, F32)] * 5 + [jax.ShapeDtypeStruct(flat, F32)] * 4
     held = pl.pallas_call(
         functools.partial(front_kernel, sizes, shape),
         out_shape=[
@@ -507,9 +514,10 @@
             jax.ShapeDtypeStruct(flat, BF16),
         ],
         in_specs=[in_hbm] * 5,
-        out_specs=[in_vmem] * 10,
+        out_specs=[in_vmem] * 11,
         scratch_shapes=[
             pltpu.VMEM((devices, half, channels), BF16),
+            pltpu.VMEM(cube, F32),
             pltpu.VMEM(w_proj.shape, BF16),
             pltpu.VMEM(w_gate.shape, BF16),
             pltpu.SMEM((length,), jnp.int32),
@@ -522,7 +530,7 @@
             collective_id=0, has_side_effects=True, vmem_limit_bytes=16 * 1024 * 1024
         ),
         name="front",
-    )(pair_own, cot_own, residue_mask, w_proj, w_gate)
+    )(*(pltpu.with_memory_space_constraint(each, pltpu.HBM) for each in (pair_own, cot_own, residue_mask, w_proj, w_gate)))
     cube_room = pltpu.VMEM(cube, F32)
     flat_room = pltpu.VMEM(flat, F32)
     turned, d_pair, g_proj, g_gate, g_out = pl.pallas_call(
@@ -537,14 +545,14 @@
         in_specs=[in_vmem] * 14,
         out_specs=[in_vmem] * 5,
         scratch_shapes=[
-            cube_room, flat_room, cube_room, cube_room,
+            flat_room, cube_room,
             cube_room, cube_room, cube_room, cube_room, flat_room,
             pltpu.VMEM((length * length, w_proj.shape[1]), BF16),
             pltpu.VMEM(flat, BF16),
         ],
         compiler_params=pltpu.CompilerParams(vmem_limit_bytes=24 * 1024 * 1024),
         name="crop",
-    )(*held, w_proj, w_gate, w_out, pair_own)
+    )(*held, w_proj, w_gate, w_out)
     return (
         turned.reshape(d_transposed.shape),
         d_pair.reshape(pair_act.shape),

time: 29.2 us -> 23.9 us (0.82)
  local copies, waits for them, and re-layouts: 4.44 us -> 0.01 us
  Pallas kernels: 23.7 us -> 23 us
    unnamed x16 -> x6, local copies, waits for them, and re-layouts: 4.44 us -> 0.01 us
    pallas_call x1, Pallas kernels: 8.48 us -> 6.91 us  [on_device_whole(): pl.pallas_call(functools.partial(crop_kernel, sizes, shape), out_shape=(j...]
    pallas_call x1, Pallas kernels: 15.2 us -> 16.1 us  [on_device_whole(): pl.pallas_call(functools.partial(front_kernel, sizes, shape), out_shape=[...]
where the time goes in v3:
time: 23.9 us; the launch traced here: 23.7 us
  Pallas kernels  23 us (96%)
  between operations  0.69 us (3%)
    pallas_call x1, Pallas kernels, on_device_whole(): pl.pallas_call(functools.partial(front_kernel, sizes, shape), out_shape=[...  16.1 us
    pallas_call x1, Pallas kernels, on_device_whole(): pl.pallas_call(functools.partial(crop_kernel, sizes, shape), out_shape=(j...  6.91 us

profile of v3, /device:TPU:0, one launch (start us, length us, event | category | flops | bytes accessed | tf_op | source)
XLA Modules:
  0.0 23.7 jit_solution(6586309913755154168)
XLA Ops:
  0.6 0.0 copy-start
  0.6 0.0 copy-start.1
  0.7 0.0 copy-start.2
  0.7 16.1 %front.1 = (bf16[16,64,128]{2,1,0:T(8,128)(2,1)S(1)}, f32[32,32,128]{2,1,0:T(8,128)S(1)}, f32[32,32,128]{2,1,0:T(8,128)S(1)}, f32[32,32,128]{2,1,0:T(8,128)S(1)}...) custom-call(bf16[64,128]{1,0:T(8,128)(2,1)} %bitcast.4, ...), custom_call_target="tpu_custom_call" | custom-call | tf_op jit(solution)/shard_map/front/pallas_call | solution.py:509
  16.8 0.0 copy-done
  16.8 0.0 copy-done.1
  16.8 0.0 copy-done.2
  16.8 6.9 %crop.1 = (bf16[64,128]{1,0:T(8,128)(2,1)}, bf16[64,128]{1,0:T(8,128)(2,1)}, f32[128,512]{1,0:T(8,128)}, f32[128,128]{1,0:T(8,128)}, f32[128,128]{1,0:T(8,128)}) custom-call(bf16[16,64,128]{2,1,0:T(8,128)(2,1)S(1)} %get-tuple-element.21.cot_all, f32[32,32,128]{2,1,0:T(8,128)S(1)} %get-tuple-element.22.pair, f32[32,32,128]{2,1,0:T(8,128)S(1)} %get-tuple-element.23.gate, ...), custom_call_target="tpu_custom_call" | custom-call | tf_op jit(solution)/shard_map/crop/pallas_call | solution.py:536
Async XLA Ops:
  0.6 16.2 %copy-start = (bf16[128,512]{1,0:T(8,128)(2,1)S(1)}, bf16[128,512]{1,0:T(8,128)(2,1)}, u32[]{:S(2)}) copy-start(bf16[128,512]{1,0:T(8,128)(2,1)} %w_proj_ref.1) | copy-start | bytes 393220
  0.6 16.2 %copy-start.1 = (bf16[128,128]{1,0:T(8,128)(2,1)S(1)}, bf16[128,128]{1,0:T(8,128)(2,1)}, u32[]{:S(2)}) copy-start(bf16[128,128]{1,0:T(8,128)(2,1)} %w_gate_ref.1) | copy-start | bytes 98308
  0.7 16.2 %copy-start.2 = (bf16[128,128]{1,0:T(8,128)(2,1)S(1)}, bf16[128,128]{1,0:T(8,128)(2,1)}, u32[]{:S(2)}) copy-start(bf16[128,128]{1,0:T(8,128)(2,1)} %w_out_ref.1) | copy-start | bytes 98308

commit v4 on v3

--- a/solution.py
+++ b/solution.py
@@ -230,7 +230,7 @@
     return lax.dot_general(a, b, (((0,), (0,)), ((), ())), preferred_element_type=F32)
 
 
-def triangle(out, entry, table, length, block=4, first=0, last=None):
+def triangle(out, entry, table, length, block=8):
     def step(at, carry):
         totals = [None] * block
         for s in range(length):
@@ -242,7 +242,7 @@
             out[at * block + q] = totals[q]
         return carry
 
-    lax.fori_loop(first, length // block if last is None else last, step, 0)
+    lax.fori_loop(0, length // block, step, 0)
 
 
 def get(ref, at, sizes, shape):
@@ -372,6 +372,37 @@
             two[rows_at] = vs * (1.0 - s)
             put(ref, at, sizes, shape, vs.astype(BF16).astype(F32))
 
+    right_flat = right.reshape(length * length, width)
+
+    def tile(q):
+        return pl.ds(pl.multiple_of(order[q] * row_block, row_block), row_block)
+
+    def cross_part(q, targets, block):
+        def step(at, carry):
+            first = order[q] * row_block + at * block
+            totals = [[None] * len(targets) for _ in range(block)]
+            for s in range(length):
+                tables = [right_by_k[s, tile(t)] for t in targets]
+                for b in range(block):
+                    entry = left[first + b, pl.ds(s, 1)]
+                    for n, table in enumerate(tables):
+                        term = entry * table
+                        totals[b][n] = term if s == 0 else totals[b][n] + term
+            for b in range(block):
+                for n, t in enumerate(targets):
+                    crossed[first + b, tile(t)] = totals[b][n]
+            return carry
+
+        lax.fori_loop(0, row_block // block, step, 0)
+
+    def cross(q):
+        start = order[q] * row_block * length
+        for k in range(length):
+            right_by_k[k, tile(q)] = right_flat[pl.ds(start + k, row_block, stride=length)]
+        cross_part(q, list(range(q + 1)), 8 if q < 2 else 4)
+        for earlier in range(q):
+            cross_part(earlier, [q], 8)
+
     send_own(0)
     send_own(1)
     pass_on(0, 0)
@@ -380,19 +411,15 @@
     front(0)
     for q in range(2, rows):
         pass_on(0, q)
+    cross(0)
     for q in range(1, rows):
         from_other(0, q)
         front(q)
-    right_flat = right.reshape(length * length, width)
-    for i in range(length):
-        right_by_k[i] = right_flat[pl.ds(i, length, stride=length)]
-    middle = length // 8
-    pass_on(1, 0)
-    pass_on(1, 1)
-    triangle(crossed, lambda a, s: left[a, pl.ds(s, 1)], right_by_k, length, last=middle)
-    for q in range(2, rows):
+        cross(q)
+        if q == rows - 2:
+            pass_on(1, 0)
+    for q in range(1, rows):
         pass_on(1, q)
-    triangle(crossed, lambda a, s: left[a, pl.ds(s, 1)], right_by_k, length, first=middle)
     for q in range(rows):
         from_other(1, q)
     for kind in (0, 1):
@@ -447,7 +474,7 @@
         g_out_ref[...] += dot_tn(unit_b, d_out_b)
         return carry
 
-    lax.fori_loop(0, rows, middle, 0)
+    lax.fori_loop(0, rows, middle, 0, unroll=True)
 
     triangle(d_left, lambda a, s: d_cross[a, pl.ds(s, 1)], right, length)
     triangle(d_right, lambda a, s: d_cross[s, pl.ds(a, 1)], left, length)
@@ -466,7 +493,7 @@
         g_gate_ref[...] += dot_tn(unit_b, gate_b)
         return carry
 
-    lax.fori_loop(0, rows, finish, 0)
+    lax.fori_loop(0, rows, finish, 0, unroll=True)
 
     share = 1.0 / length
     g_proj_ref[...] = g_proj_ref[...] * share

time: 23.9 us -> 22.7 us (0.950)
  Pallas kernels: 23 us -> 21.9 us
    pallas_call x1, Pallas kernels: 6.91 us -> 5.4 us  [on_device_whole(): pl.pallas_call(functools.partial(crop_kernel, sizes, shape), out_shape=(j...]
    pallas_call x1, Pallas kernels: 16.1 us -> 16.5 us  [on_device_whole(): pl.pallas_call(functools.partial(front_kernel, sizes, shape), out_shape=[...]
where the time goes in v4:
time: 22.7 us; the launch traced here: 22.6 us
  Pallas kernels  21.9 us (96%)
  between operations  0.69 us (3%)
    pallas_call x1, Pallas kernels, on_device_whole(): pl.pallas_call(functools.partial(front_kernel, sizes, shape), out_shape=[...  16.5 us
    pallas_call x1, Pallas kernels, on_device_whole(): pl.pallas_call(functools.partial(crop_kernel, sizes, shape), out_shape=(j...  5.4 us

profile of v4, /device:TPU:0, one launch (start us, length us, event | category | flops | bytes accessed | tf_op | source)
XLA Modules:
  0.0 22.6 jit_solution(7811393593021250188)
XLA Ops:
  0.6 0.0 copy-start
  0.6 0.0 copy-start.1
  0.7 0.0 copy-start.2
  0.7 16.5 %front.1 = (bf16[16,64,128]{2,1,0:T(8,128)(2,1)S(1)}, f32[32,32,128]{2,1,0:T(8,128)S(1)}, f32[32,32,128]{2,1,0:T(8,128)S(1)}, f32[32,32,128]{2,1,0:T(8,128)S(1)}...) custom-call(bf16[64,128]{1,0:T(8,128)(2,1)} %bitcast.4, ...), custom_call_target="tpu_custom_call" | custom-call | tf_op jit(solution)/shard_map/front/pallas_call | solution.py:536
  17.1 0.0 copy-done
  17.1 0.0 copy-done.1
  17.1 0.0 copy-done.2
  17.2 5.4 %crop.1 = (bf16[64,128]{1,0:T(8,128)(2,1)}, bf16[64,128]{1,0:T(8,128)(2,1)}, f32[128,512]{1,0:T(8,128)}, f32[128,128]{1,0:T(8,128)}, f32[128,128]{1,0:T(8,128)}) custom-call(bf16[16,64,128]{2,1,0:T(8,128)(2,1)S(1)} %get-tuple-element.21.cot_all, f32[32,32,128]{2,1,0:T(8,128)S(1)} %get-tuple-element.22.pair, f32[32,32,128]{2,1,0:T(8,128)S(1)} %get-tuple-element.23.gate, ...), custom_call_target="tpu_custom_call" | custom-call | tf_op jit(solution)/shard_map/crop/pallas_call | solution.py:563
Async XLA Ops:
  0.6 16.5 %copy-start = (bf16[128,512]{1,0:T(8,128)(2,1)S(1)}, bf16[128,512]{1,0:T(8,128)(2,1)}, u32[]{:S(2)}) copy-start(bf16[128,512]{1,0:T(8,128)(2,1)} %w_proj_ref.1) | copy-start | bytes 393220
  0.6 16.5 %copy-start.1 = (bf16[128,128]{1,0:T(8,128)(2,1)S(1)}, bf16[128,128]{1,0:T(8,128)(2,1)}, u32[]{:S(2)}) copy-start(bf16[128,128]{1,0:T(8,128)(2,1)} %w_gate_ref.1) | copy-start | bytes 98308
  0.7 16.5 %copy-start.2 = (bf16[128,128]{1,0:T(8,128)(2,1)S(1)}, bf16[128,128]{1,0:T(8,128)(2,1)}, u32[]{:S(2)}) copy-start(bf16[128,128]{1,0:T(8,128)(2,1)} %w_out_ref.1) | copy-start | bytes 98308

commit v5 on v3

--- a/solution.py
+++ b/solution.py
@@ -230,7 +230,7 @@
     return lax.dot_general(a, b, (((0,), (0,)), ((), ())), preferred_element_type=F32)
 
 
-def triangle(out, entry, table, length, block=4, first=0, last=None):
+def triangle(out, entry, table, length, block=8):
     def step(at, carry):
         totals = [None] * block
         for s in range(length):
@@ -242,7 +242,7 @@
             out[at * block + q] = totals[q]
         return carry
 
-    lax.fori_loop(first, length // block if last is None else last, step, 0)
+    lax.fori_loop(0, length // block, step, 0)
 
 
 def get(ref, at, sizes, shape):
@@ -269,9 +269,9 @@
 
 def front_kernel(
     sizes, shape,
-    pair_hbm, cot_hbm, mask_hbm, w_proj_hbm, w_gate_hbm,
-    cot_all, pair, gate, left, right, crossed, l_one, l_two, r_one, r_two, normed,
-    pair_all, right_by_k, w_proj, w_gate, mask_row, mask, own_sem, send_sem, recv_sem,
+    pair_hbm, cot_hbm, mask_hbm, w_proj_hbm, w_gate_hbm, w_out_hbm,
+    cot_all, pair, gate, left, right, unit_x, scale_x, gated, l_one, l_two, r_one, r_two, normed,
+    pair_all, right_by_k, crossed, w_proj, w_gate, w_out, mask_row, mask, own_sem, send_sem, recv_sem,
 ):
     rows, subs, pairs = sizes
     row_block, col_block, width = shape
@@ -297,6 +297,7 @@
         pltpu.make_async_copy(mask_hbm, mask_row, own_sem.at[2]),
         pltpu.make_async_copy(w_proj_hbm, w_proj, own_sem.at[3]),
         pltpu.make_async_copy(w_gate_hbm, w_gate, own_sem.at[4]),
+        pltpu.make_async_copy(w_out_hbm, w_out, own_sem.at[5]),
     ]
     for one in local:
         one.start()
@@ -313,7 +314,7 @@
         col_mask = jnp.where(place == i, mask_row[i].astype(F32), col_mask)
     for i in range(length):
         mask[i] = col_mask * mask_row[i].astype(F32)
-    for one in (local[0], local[1], local[3], local[4]):
+    for one in local[:2] + local[3:]:
         one.wait()
     pl.semaphore_wait(barrier, len(far_first) + 1)
 
@@ -352,47 +353,91 @@
         for sub in (x, 1 - x):
             copy(kind, slot(order[q], sub, 1 - c), 0, other).wait_recv()
 
-    def front(q):
-        at = order[q]
-        rows_at = pl.ds(pl.multiple_of(at * band, band), band)
-        values = pair_all[pl.ds(at * col_groups, col_groups)].reshape(band, width).astype(F32)
-        put(pair, at, sizes, shape, values)
+    def front(chunks):
+        blocks = [(order[q], sub * pairs + core) for q, core in chunks for sub in range(subs)]
+
+        def place_of(at, g):
+            rows_at = pl.ds(pl.multiple_of((at * col_groups + g) * half, half), half)
+            cols = pl.ds(pl.multiple_of(g * col_block, col_block), col_block)
+            return rows_at, (pl.ds(pl.multiple_of(at * row_block, row_block), row_block), cols)
+
+        places = [place_of(at, g) for at, g in blocks]
+
+        def put_flat(ref, values):
+            for n, (rows_at, _) in enumerate(places):
+                ref[rows_at] = values[n * half : (n + 1) * half]
+
+        def put_cube(ref, values):
+            for n, (_, where) in enumerate(places):
+                ref[where] = values[n * half : (n + 1) * half].reshape(row_block, col_block, width)
+
+        values = jnp.concatenate([pair_all[at * col_groups + g] for at, g in blocks], axis=0).astype(F32)
+        put_cube(pair, values)
         unit, _ = norm_rows(values)
         unit_b = unit.astype(BF16)
-        normed[rows_at] = unit_b
-        m = get(mask, at, sizes, shape)
-        put(gate, at, sizes, shape, sigmoid(dot_nn(unit_b, w_gate[...])))
+        put_flat(normed, unit_b)
+        m = jnp.concatenate([mask[where].reshape(half, width) for _, where in places], axis=0)
+        put_cube(gate, sigmoid(dot_nn(unit_b, w_gate[...])))
         projected = dot_nn(unit_b, w_proj[...])
         for base, ref, one, two in ((0, left, l_one, l_two), (2, right, r_one, r_two)):
             s = sigmoid(projected[:, base * width : (base + 1) * width])
             v = projected[:, (base + 1) * width : (base + 2) * width]
             sm = s * m
             vs = v * sm
-            one[rows_at] = sm
-            two[rows_at] = vs * (1.0 - s)
-            put(ref, at, sizes, shape, vs.astype(BF16).astype(F32))
+            put_flat(one, sm)
+            put_flat(two, vs * (1.0 - s))
+            put_cube(ref, vs.astype(BF16).astype(F32))
+
+    right_flat = right.reshape(length * length, width)
+
+    def cross(core, more):
+        ks = [(sub * pairs + core) * col_block + at for sub in range(subs) for at in range(col_block)]
+        for k in ks:
+            right_by_k[k] = right_flat[pl.ds(k, length, stride=length)]
+
+        def step(at, carry):
+            totals = [crossed[at * 8 + q] if more else None for q in range(8)]
+            for k in ks:
+                rows_k = right_by_k[k]
+                for q in range(8):
+                    term = left[at * 8 + q, pl.ds(k, 1)] * rows_k
+                    totals[q] = term if totals[q] is None else totals[q] + term
+            for q in range(8):
+                crossed[at * 8 + q] = totals[q]
+            return carry
+
+        lax.fori_loop(0, length // 8, step, 0)
 
     send_own(0)
     send_own(1)
     pass_on(0, 0)
-    pass_on(0, 1)
     from_other(0, 0)
-    front(0)
-    for q in range(2, rows):
+    front([(0, c), (0, 1 - c)])
+    for q in range(1, rows):
         pass_on(0, q)
+    front([(q, c) for q in range(1, rows)])
+    cross(c, False)
+    pass_on(1, 0)
+    pass_on(1, 1)
     for q in range(1, rows):
         from_other(0, q)
-        front(q)
-    right_flat = right.reshape(length * length, width)
-    for i in range(length):
-        right_by_k[i] = right_flat[pl.ds(i, length, stride=length)]
-    middle = length // 8
-    pass_on(1, 0)
-    pass_on(1, 1)
-    triangle(crossed, lambda a, s: left[a, pl.ds(s, 1)], right_by_k, length, last=middle)
+    front([(q, 1 - c) for q in range(1, rows)])
     for q in range(2, rows):
         pass_on(1, q)
-    triangle(crossed, lambda a, s: left[a, pl.ds(s, 1)], right_by_k, length, first=middle)
+    cross(1 - c, True)
+
+    def second_norm(at, carry):
+        here = pl.ds(at * row_block, row_block)
+        in_cube = (row_block, length, width)
+        held = crossed[here].reshape(band, width).astype(BF16).astype(F32)
+        each, scale_rows = norm_rows(held)
+        out_proj = dot_nn(each.astype(BF16), w_out[...])
+        unit_x[here] = each.reshape(in_cube)
+        scale_x[here] = jnp.broadcast_to(scale_rows, each.shape).reshape(in_cube)
+        gated[here] = (gate[here].reshape(band, width) * out_proj).reshape(in_cube)
+        return carry
+
+    lax.fori_loop(0, rows, second_norm, 0, unroll=True)
     for q in range(rows):
         from_other(1, q)
     for kind in (0, 1):
@@ -402,11 +447,11 @@
 
 def crop_kernel(
     sizes, shape,
-    cot_all, pair, gate, left, right, crossed, l_one, l_two, r_one, r_two, normed,
+    cot_all, pair, gate, left, right, unit_x, scale_x, gated, l_one, l_two, r_one, r_two, normed,
     w_proj_ref, w_gate_ref, w_out_ref,
     turned_ref, d_pair_ref, g_proj_ref, g_gate_ref, g_out_ref,
     cot_flat, d_up,
-    d_cross, d_left, d_right, d_gate, up_flat, d_proj, d_gate_b,
+    d_cross, d_left, d_right, d_gate, d_proj, d_gate_b,
 ):
     rows, subs, pairs = sizes
     row_block, col_block, width = shape
@@ -431,23 +476,18 @@
         def flat(ref):
             return ref[here].reshape(band, width)
 
-        unit, scale = norm_rows(flat(crossed).astype(BF16).astype(F32))
-        unit_b = unit.astype(BF16)
-        w_out = w_out_ref[...]
-        out_proj = dot_nn(unit_b, w_out)
+        unit = flat(unit_x)
         g = flat(gate)
         up = flat(d_up)
-        gated = g * out_proj
-        up_flat[pl.ds(pl.multiple_of(at * band, band), band)] = flat(pair) + gated
         d_out_b = (g * up).astype(BF16)
-        d_gate[here] = (gated * up * (1.0 - g)).reshape(row_block, length, width)
-        d_unit = dot_nt(d_out_b, w_out)
-        back = norm_rows_back(unit, scale, d_unit)
+        d_gate[here] = (flat(gated) * up * (1.0 - g)).reshape(row_block, length, width)
+        d_unit = dot_nt(d_out_b, w_out_ref[...])
+        back = norm_rows_back(unit, flat(scale_x), d_unit)
         d_cross[here] = back.astype(BF16).astype(F32).reshape(row_block, length, width)
-        g_out_ref[...] += dot_tn(unit_b, d_out_b)
+        g_out_ref[...] += dot_tn(unit.astype(BF16), d_out_b)
         return carry
 
-    lax.fori_loop(0, rows, middle, 0)
+    lax.fori_loop(0, rows, middle, 0, unroll=True)
 
     triangle(d_left, lambda a, s: d_cross[a, pl.ds(s, 1)], right, length)
     triangle(d_right, lambda a, s: d_cross[s, pl.ds(a, 1)], left, length)
@@ -466,7 +506,7 @@
         g_gate_ref[...] += dot_tn(unit_b, gate_b)
         return carry
 
-    lax.fori_loop(0, rows, finish, 0)
+    lax.fori_loop(0, rows, finish, 0, unroll=True)
 
     share = 1.0 / length
     g_proj_ref[...] = g_proj_ref[...] * share
@@ -487,9 +527,9 @@
 
     turned_rows = half // length
     for q in range(turned_rows):
-        turned_ref[q * length : (q + 1) * length] = up_flat[
-            pl.ds(own * turned_rows + q, length, stride=length)
-        ].astype(BF16)
+        rows_at = pl.ds(own * turned_rows + q, length, stride=length)
+        turned = pair.reshape(length * length, width)[rows_at] + gated.reshape(length * length, width)[rows_at]
+        turned_ref[q * length : (q + 1) * length] = turned.astype(BF16)
 
 
 def on_device_whole(sizes, pair_act, residue_mask, w_proj, w_gate, w_out, d_transposed):
@@ -505,7 +545,7 @@
     in_hbm = pl.BlockSpec(memory_space=pltpu.HBM)
     cube = (length, length, channels)
     flat = (length * length, channels)
-    kept = [jax.ShapeDtypeStruct(cube, F32)] * 5 + [jax.ShapeDtypeStruct(flat, F32)] * 4
+    kept = [jax.ShapeDtypeStruct(cube, F32)] * 7 + [jax.ShapeDtypeStruct(flat, F32)] * 4
     held = pl.pallas_call(
         functools.partial(front_kernel, sizes, shape),
         out_shape=[
@@ -513,16 +553,18 @@
             *kept,
             jax.ShapeDtypeStruct(flat, BF16),
         ],
-        in_specs=[in_hbm] * 5,
-        out_specs=[in_vmem] * 11,
+        in_specs=[in_hbm] * 6,
+        out_specs=[in_vmem] * 13,
         scratch_shapes=[
             pltpu.VMEM((devices, half, channels), BF16),
             pltpu.VMEM(cube, F32),
+            pltpu.VMEM(cube, F32),
             pltpu.VMEM(w_proj.shape, BF16),
             pltpu.VMEM(w_gate.shape, BF16),
+            pltpu.VMEM(w_out.shape, BF16),
             pltpu.SMEM((length,), jnp.int32),
             pltpu.VMEM(cube, F32),
-            pltpu.SemaphoreType.DMA((5,)),
+            pltpu.SemaphoreType.DMA((6,)),
             pltpu.SemaphoreType.DMA((2, devices)),
             pltpu.SemaphoreType.DMA((2, devices)),
         ],
@@ -530,7 +572,7 @@
             collective_id=0, has_side_effects=True, vmem_limit_bytes=16 * 1024 * 1024
         ),
         name="front",
-    )(*(pltpu.with_memory_space_constraint(each, pltpu.HBM) for each in (pair_own, cot_own, residue_mask, w_proj, w_gate)))
+    )(*(pltpu.with_memory_space_constraint(each, pltpu.HBM) for each in (pair_own, cot_own, residue_mask, w_proj, w_gate, w_out)))
     cube_room = pltpu.VMEM(cube, F32)
     flat_room = pltpu.VMEM(flat, F32)
     turned, d_pair, g_proj, g_gate, g_out = pl.pallas_call(
@@ -542,11 +584,11 @@
             jax.ShapeDtypeStruct(w_gate.shape, F32),
             jax.ShapeDtypeStruct(w_out.shape, F32),
         ),
-        in_specs=[in_vmem] * 14,
+        in_specs=[in_vmem] * 16,
         out_specs=[in_vmem] * 5,
         scratch_shapes=[
             flat_room, cube_room,
-            cube_room, cube_room, cube_room, cube_room, flat_room,
+            cube_room, cube_room, cube_room, cube_room,
             pltpu.VMEM((length * length, w_proj.shape[1]), BF16),
             pltpu.VMEM(flat, BF16),
         ],
@@ -566,7 +608,7 @@
     row_block, col_block, channels = pair_act.shape
     length = sizes[0] * row_block
     fits = (
-        length <= 32
+        1 < sizes[0] and length <= 32
         and row_block % 8 == 0
         and col_block % 8 == 0
         and sizes[1:] == (2, 2)

time: 23.9 us -> 21.2 us (0.89)
  Pallas kernels: 23 us -> 20.4 us
    pallas_call x1, Pallas kernels: 6.91 us -> 4.94 us  [on_device_whole(): pl.pallas_call(functools.partial(crop_kernel, sizes, shape), out_shape=(j...]
    pallas_call x1, Pallas kernels: 16.1 us -> 15.4 us  [on_device_whole(): pl.pallas_call(functools.partial(front_kernel, sizes, shape), out_shape=[...]
where the time goes in v5:
time: 21.2 us; the launch traced here: 21.1 us
  Pallas kernels  20.4 us (96%)
  between operations  0.69 us (3%)
    pallas_call x1, Pallas kernels, on_device_whole(): pl.pallas_call(functools.partial(front_kernel, sizes, shape), out_shape=[...  15.4 us
    pallas_call x1, Pallas kernels, on_device_whole(): pl.pallas_call(functools.partial(crop_kernel, sizes, shape), out_shape=(j...  4.94 us

profile of v5, /device:TPU:0, one launch (start us, length us, event | category | flops | bytes accessed | tf_op | source)
XLA Modules:
  0.0 21.1 jit_solution(14416399386819911747)
XLA Ops:
  0.6 0.0 copy-start
  0.6 0.0 copy-start.1
  0.7 0.0 copy-start.2
  0.7 15.4 %front.1 = (bf16[16,64,128]{2,1,0:T(8,128)(2,1)S(1)}, f32[32,32,128]{2,1,0:T(8,128)S(1)}, f32[32,32,128]{2,1,0:T(8,128)S(1)}, f32[32,32,128]{2,1,0:T(8,128)S(1)}...) custom-call(bf16[64,128]{1,0:T(8,128)(2,1)} %bitcast.4, ...), custom_call_target="tpu_custom_call" | custom-call | tf_op jit(solution)/shard_map/front/pallas_call | solution.py:549
  16.1 0.0 copy-done
  16.1 0.0 copy-done.1
  16.1 0.0 copy-done.2
  16.1 4.9 %crop.1 = (bf16[64,128]{1,0:T(8,128)(2,1)}, bf16[64,128]{1,0:T(8,128)(2,1)}, f32[128,512]{1,0:T(8,128)}, f32[128,128]{1,0:T(8,128)}, f32[128,128]{1,0:T(8,128)}) custom-call(bf16[16,64,128]{2,1,0:T(8,128)(2,1)S(1)} %get-tuple-element.23.cot_all, f32[32,32,128]{2,1,0:T(8,128)S(1)} %get-tuple-element.24.pair, f32[32,32,128]{2,1,0:T(8,128)S(1)} %get-tuple-element.25.gate, ...), custom_call_target="tpu_custom_call" | custom-call | tf_op jit(solution)/shard_map/crop/pallas_call | solution.py:578
Async XLA Ops:
  0.6 15.5 %copy-start = (bf16[128,512]{1,0:T(8,128)(2,1)S(1)}, bf16[128,512]{1,0:T(8,128)(2,1)}, u32[]{:S(2)}) copy-start(bf16[128,512]{1,0:T(8,128)(2,1)} %w_proj_ref.1) | copy-start | bytes 393220
  0.6 15.5 %copy-start.1 = (bf16[128,128]{1,0:T(8,128)(2,1)S(1)}, bf16[128,128]{1,0:T(8,128)(2,1)}, u32[]{:S(2)}) copy-start(bf16[128,128]{1,0:T(8,128)(2,1)} %w_gate_ref.1) | copy-start | bytes 98308
  0.7 15.5 %copy-start.2 = (bf16[128,128]{1,0:T(8,128)(2,1)S(1)}, bf16[128,128]{1,0:T(8,128)(2,1)}, u32[]{:S(2)}) copy-start(bf16[128,128]{1,0:T(8,128)(2,1)} %w_out_ref.1) | copy-start | bytes 98308

commit v6 on v5

--- a/solution.py
+++ b/solution.py
@@ -230,13 +230,13 @@
     return lax.dot_general(a, b, (((0,), (0,)), ((), ())), preferred_element_type=F32)
 
 
-def triangle(out, entry, table, length, block=8):
+def triangle(out, entries, table, length, block=8):
     def step(at, carry):
         totals = [None] * block
         for s in range(length):
             rows = table[s]
-            for q in range(block):
-                term = entry(at * block + q, s) * rows
+            for q, each in enumerate(entries(at, s)):
+                term = each * rows
                 totals[q] = term if s == 0 else totals[q] + term
         for q in range(block):
             out[at * block + q] = totals[q]
@@ -489,8 +489,16 @@
 
     lax.fori_loop(0, rows, middle, 0, unroll=True)
 
-    triangle(d_left, lambda a, s: d_cross[a, pl.ds(s, 1)], right, length)
-    triangle(d_right, lambda a, s: d_cross[s, pl.ds(a, 1)], left, length)
+
+    def entries_left(at, s):
+        return [d_cross[at * 8 + q, pl.ds(s, 1)] for q in range(8)]
+
+    def entries_right(at, s):
+        tile = d_cross[s, pl.ds(pl.multiple_of(at * 8, 8), 8)]
+        return [tile[q : q + 1] for q in range(8)]
+
+    triangle(d_left, entries_left, right, length)
+    triangle(d_right, entries_right, left, length)
 
     def finish(at, carry):
         rows_at = pl.ds(pl.multiple_of(at * band, band), band)

time: 21.2 us -> 21.2 us (level)
  no operation moved by 1% of the time
where the time goes in v6:
time: 21.2 us; the launch traced here: 21.1 us
  Pallas kernels  20.4 us (96%)
  between operations  0.69 us (3%)
    pallas_call x1, Pallas kernels, on_device_whole(): pl.pallas_call(functools.partial(front_kernel, sizes, shape), out_shape=[...  15.4 us
    pallas_call x1, Pallas kernels, on_device_whole(): pl.pallas_call(functools.partial(crop_kernel, sizes, shape), out_shape=(j...  4.95 us

profile of v6, /device:TPU:0, one launch (start us, length us, event | category | flops | bytes accessed | tf_op | source)
XLA Modules:
  0.0 21.1 jit_solution(5031948521610940815)
XLA Ops:
  0.6 0.0 copy-start
  0.6 0.0 copy-start.1
  0.7 0.0 copy-start.2
  0.7 15.4 %front.1 = (bf16[16,64,128]{2,1,0:T(8,128)(2,1)S(1)}, f32[32,32,128]{2,1,0:T(8,128)S(1)}, f32[32,32,128]{2,1,0:T(8,128)S(1)}, f32[32,32,128]{2,1,0:T(8,128)S(1)}...) custom-call(bf16[64,128]{1,0:T(8,128)(2,1)} %bitcast.4, ...), custom_call_target="tpu_custom_call" | custom-call | tf_op jit(solution)/shard_map/front/pallas_call | solution.py:557
  16.1 0.0 copy-done
  16.1 0.0 copy-done.1
  16.1 0.0 copy-done.2
  16.1 4.9 %crop.1 = (bf16[64,128]{1,0:T(8,128)(2,1)}, bf16[64,128]{1,0:T(8,128)(2,1)}, f32[128,512]{1,0:T(8,128)}, f32[128,128]{1,0:T(8,128)}, f32[128,128]{1,0:T(8,128)}) custom-call(bf16[16,64,128]{2,1,0:T(8,128)(2,1)S(1)} %get-tuple-element.23.cot_all, f32[32,32,128]{2,1,0:T(8,128)S(1)} %get-tuple-element.24.pair, f32[32,32,128]{2,1,0:T(8,128)S(1)} %get-tuple-element.25.gate, ...), custom_call_target="tpu_custom_call" | custom-call | tf_op jit(solution)/shard_map/crop/pallas_call | solution.py:586
Async XLA Ops:
  0.6 15.5 %copy-start = (bf16[128,512]{1,0:T(8,128)(2,1)S(1)}, bf16[128,512]{1,0:T(8,128)(2,1)}, u32[]{:S(2)}) copy-start(bf16[128,512]{1,0:T(8,128)(2,1)} %w_proj_ref.1) | copy-start | bytes 393220
  0.6 15.5 %copy-start.1 = (bf16[128,128]{1,0:T(8,128)(2,1)S(1)}, bf16[128,128]{1,0:T(8,128)(2,1)}, u32[]{:S(2)}) copy-start(bf16[128,128]{1,0:T(8,128)(2,1)} %w_gate_ref.1) | copy-start | bytes 98308
  0.7 15.5 %copy-start.2 = (bf16[128,128]{1,0:T(8,128)(2,1)S(1)}, bf16[128,128]{1,0:T(8,128)(2,1)}, u32[]{:S(2)}) copy-start(bf16[128,128]{1,0:T(8,128)(2,1)} %w_out_ref.1) | copy-start | bytes 98308
